TPU v7x, 256 devices: a whole 4x4x8 slice. The times are simulated.
256 devices in a mesh: dp: 16 (over z, core), tp: 16 (over x, y).
Axes of the slice: x: 4, y: 4, z: 8, core: 2. Of those that a mesh axis runs over, the one named last changes fastest.
Arguments:
- token_states: bfloat16 [256, 7168], P('dp', 'tp'), may hold values from -12 to 12
- queries: bfloat16 [4, 256, 64, 576], P(None, ('dp', 'tp')), may hold values from -57 to 57
- kv_cache: bfloat16 [256, 4096, 576], P(('dp', 'tp')), may hold values from -6 to 6
- lengths: int32 [256], P(('dp', 'tp')), may hold values from 1 to 4096, 524288 in all
- attn_gain: float32 [7168], P('tp'), may hold values from 0.5 to 1.5
- kv_gain: float32 [512], replicated, may hold values from 0.5 to 1.5
- w_latent: bfloat16 [7168, 576], P('tp'), may hold values from -0.0625 to 0.0625
- w_out: bfloat16 [32768, 7168], P('dp', 'tp'), may hold values from -0.03125 to 0.03125
- mlp_gain: float32 [7168], P('tp'), may hold values from 0.5 to 1.5
- w_gate_up: bfloat16 [2, 7168, 18432], P(None, 'tp', 'dp'), may hold values from -0.0625 to 0.0625
- w_down: bfloat16 [18432, 7168], P('dp', 'tp'), may hold values from -0.046875 to 0.046875
Outputs:
- mixed: bfloat16 [4, 256, 7168], P(None, 'dp', 'tp')
- latents: bfloat16 [4, 256, 576], P(None, ('dp', 'tp'))
Inputs may be any that keep to these rules, and one draw needn't show every extreme that they name: `lengths`: some user holds exactly 4096 cached tokens.
All inputs are finite; a program needn't handle non-finite values. No bound on the sum of `lengths` on one device may be relied on, other than what follows from the above.
Results may differ from a plain program's by a relative error of at most 0.03.
Values may be sent and summed in bfloat16 or wider, within the bound.
A program may use at most 64 MiB of HBM per device.

v0:
```python
import jax
import jax.numpy as jnp
from jax import lax
from jax.sharding import PartitionSpec as P

D = 7168


norm_eps = 1e-06
score_scale = 192.0 ** (-0.5)


def rotate_pairs(rope_part, positions):
    half_width = rope_part.shape[1] // 2
    frequency = 10000.0 ** (-jnp.arange(half_width, dtype=jnp.float32) / half_width)
    angles = positions.astype(jnp.float32)[:, None] * frequency[None, :]
    cosine = jnp.cos(angles)
    sine_part = jnp.sin(angles)
    front_half = rope_part[:, :half_width]
    back_half = rope_part[:, half_width:]
    return jnp.concatenate(
        [front_half * cosine - back_half * sine_part, front_half * sine_part + back_half * cosine],
        axis=1,
    )


def finish_latent(raw_latent, inverse, kv_gain, positions):
    lat_width = kv_gain.shape[0]
    scaled_raw = raw_latent * inverse[:, None]
    content = scaled_raw[:, :lat_width]
    content = (
        content * lax.rsqrt(jnp.mean(content * content, axis=1, keepdims=True) + norm_eps) * kv_gain
    )
    return jnp.concatenate(
        [content, rotate_pairs(scaled_raw[:, lat_width:], positions)], axis=1
    ).astype(jnp.bfloat16)


def attend_local(query_block, kv_cache, fresh_keys, lengths, lat_width):
    cached = (
        jnp.einsum("uhk,ulk->uhl", query_block, kv_cache, preferred_element_type=jnp.float32)
        * score_scale
    )
    usable = lax.broadcasted_iota(jnp.int32, (1, 1, kv_cache.shape[1]), 2) < lengths[:, None, None]
    cached = jnp.where(usable, cached, -jnp.inf)
    recent = (
        jnp.einsum("uhk,ujk->uhj", query_block, fresh_keys, preferred_element_type=jnp.float32)
        * score_scale
    )
    highest = jnp.maximum(jnp.max(cached, axis=2), jnp.max(recent, axis=2))
    weight_old = jnp.exp(cached - highest[:, :, None])
    weight_new = jnp.exp(recent - highest[:, :, None])
    denominator = jnp.sum(weight_old, axis=2) + jnp.sum(weight_new, axis=2)
    prob_old = (weight_old / denominator[:, :, None]).astype(jnp.bfloat16)
    prob_new = (weight_new / denominator[:, :, None]).astype(jnp.bfloat16)
    mixed_heads = jnp.einsum(
        "uhl,ulc->uhc", prob_old, kv_cache[:, :, :lat_width], preferred_element_type=jnp.float32
    )
    mixed_heads = mixed_heads + jnp.einsum(
        "uhj,ujc->uhc", prob_new, fresh_keys[:, :, :lat_width], preferred_element_type=jnp.float32
    )
    return mixed_heads.astype(jnp.bfloat16).reshape(query_block.shape[0], -1)


def body(
    token_states,
    queries,
    kv_cache,
    lengths,
    attn_gain,
    kv_gain,
    w_latent,
    w_out,
    mlp_gain,
    w_gate_up,
    w_down,
):
    user_count = kv_cache.shape[0]
    lat_width = kv_gain.shape[0]
    ff_width = w_down.shape[0]
    tp_count = lax.axis_size("tp")
    tp_rank = lax.axis_index("tp")
    fresh_list = []
    mixed_steps = []
    latent_steps = []
    current_rows = token_states
    for step_index in range(queries.shape[0]):
        states = current_rows.astype(jnp.float32)
        scaled = (states * attn_gain).astype(jnp.bfloat16)
        partial_latent = jnp.dot(scaled, w_latent, preferred_element_type=jnp.float32)
        squares = jnp.sum(states * states, axis=1)
        all_squares = lax.psum(squares, "tp")
        own_squares = lax.dynamic_slice_in_dim(all_squares, tp_rank * user_count, user_count, 0)
        raw_latent = lax.psum_scatter(
            partial_latent.astype(jnp.bfloat16), "tp", scatter_dimension=0, tiled=True
        ).astype(jnp.float32)
        inverse = lax.rsqrt(own_squares / D + norm_eps)
        latent = finish_latent(raw_latent, inverse, kv_gain, lengths + step_index)
        latent_steps.append(latent)
        fresh_list.append(latent)
        fresh_keys = jnp.stack(fresh_list, axis=1)
        head_outputs = attend_local(queries[step_index], kv_cache, fresh_keys, lengths, lat_width)
        grouped = lax.all_gather(head_outputs, "tp", axis=0, tiled=True)
        all_heads = lax.all_to_all(grouped, "dp", split_axis=1, concat_axis=0, tiled=True)
        attn_out = lax.psum_scatter(
            jnp.dot(all_heads, w_out, preferred_element_type=jnp.float32).astype(jnp.bfloat16),
            "dp",
            scatter_dimension=0,
            tiled=True,
        ).astype(jnp.float32)
        residual = states + attn_out
        mix_squares = lax.psum(jnp.sum(residual * residual, axis=1), "tp")
        normed = (residual * lax.rsqrt(mix_squares / D + norm_eps)[:, None] * mlp_gain).astype(
            jnp.bfloat16
        )
        every_row = lax.all_gather(normed, "dp", axis=0, tiled=True)
        gate_and_up = jnp.einsum(
            "rk,gkf->rgf", every_row, w_gate_up, preferred_element_type=jnp.float32
        )
        gate_up = lax.psum_scatter(
            gate_and_up.reshape(every_row.shape[0] // tp_count * lax.axis_size("tp"), -1).astype(
                jnp.bfloat16
            ),
            "tp",
            scatter_dimension=0,
            tiled=True,
        ).astype(jnp.float32)
        hidden = (jax.nn.silu(gate_up[:, :ff_width]) * gate_up[:, ff_width:]).astype(jnp.bfloat16)
        hidden_all = lax.all_gather(hidden, "tp", axis=0, tiled=True)
        down_out = lax.psum_scatter(
            jnp.dot(hidden_all, w_down, preferred_element_type=jnp.float32).astype(jnp.bfloat16),
            "dp",
            scatter_dimension=0,
            tiled=True,
        ).astype(jnp.float32)
        current_rows = (residual + down_out).astype(jnp.bfloat16)
        mixed_steps.append(current_rows)
    return (jnp.stack(mixed_steps, axis=0), jnp.stack(latent_steps, axis=0))


def solution(mesh):
    placed = (
        P("dp", "tp"),
        P(None, ("dp", "tp"), None, None),
        P(("dp", "tp"), None, None),
        P(("dp", "tp")),
        P("tp"),
        P(),
        P("tp", None),
        P("dp", "tp"),
        P("tp"),
        P(None, "tp", "dp"),
        P("dp", "tp"),
    )
    return jax.shard_map(
        body,
        mesh=mesh,
        in_specs=placed,
        out_specs=(P(None, "dp", "tp"), P(None, ("dp", "tp"), None)),
        check_vma=False,
    )
```

profile of v0, /device:TPU:32, one launch (start us, length us, event | category | flops | bytes accessed | tf_op | source)
XLA Modules:
  0.0 1952.2 jit_solution(3175238580407322800)
XLA Ops:
  8.2 40.7 %psum.56 = f32[16]{0:T(128)S(1)} all-reduce(f32[16]{0:T(128)S(1)} %fusion.91), channel_id=1, replica_groups=mesh['dp'=16,'tp'=16] {'tp'}, use_global_device_ids=true, to_apply=%region_3.0 | all-reduce | flops 16 | bytes 128 | tf_op jit(solution)/shard_map/psum | solution.py:92
  51.4 69.6 %all-reduce = bf16[16,576]{1,0:T(8,128)(2,1)S(1)} all-reduce(bf16[16,576]{1,0:T(8,128)(2,1)S(1)} %convolution_convert_fusion.15), channel_id=2, replica_groups=mesh['dp'=16,'tp'=16] {'tp'}, use_global_device_ids=true, to_apply=%region_1.0.clone | all-reduce | flops 9216 | bytes 36864
  133.0 47.6 %all-gather.9.cloned.1.call-done = bf16[16,1,32768]{2,1,0:T(2,128)(2,1)} async-done(((bf16[1,1,32768]{2,1,0:T(2,128)(2,1)}), bf16[16,1,32768]{2,1,0:T(2,128)(2,1)}) %all-gather.9.cloned.1.call-update) | async-done | bytes 1048592 | tf_op jit(solution)/shard_map/all_gather | solution.py:103
  180.5 7.7 reduce.39
  188.4 33.0 %all_to_all.76 = bf16[16,16,2048]{2,0,1:T(8,128)(2,1)S(1)} all-to-all(bf16[16,16,2048]{2,0,1:T(8,128)(2,1)S(1)} %bitcast.247), channel_id=1, replica_groups=mesh['dp'=16,'tp'=16] {'dp'}, dimensions={1} | all-to-all | bytes 2097152 | tf_op jit(solution)/shard_map/all_to_all | solution.py:104
  222.9 51.0 %reduce-scatter.21.cloned.1.call-done = bf16[16,448]{1,0:T(8,128)(2,1)} async-done(((bf16[256,448]{1,0:T(8,128)(2,1)}), bf16[16,448]{1,0:T(8,128)(2,1)}) %reduce-scatter.21.cloned.1.call-update) | async-done | bytes 14352 | tf_op jit(solution)/shard_map/reduce_scatter | solution.py:105
  274.7 40.3 %psum.57 = f32[16]{0:T(128)S(1)} all-reduce(f32[16]{0:T(128)S(1)} %multiply_reduce_fusion.3), channel_id=1, replica_groups=mesh['dp'=16,'tp'=16] {'tp'}, use_global_device_ids=true, to_apply=%region_8.9 | all-reduce | flops 16 | bytes 128 | tf_op jit(solution)/shard_map/psum | solution.py:112
  315.9 18.6 all_gather.37
  339.1 71.9 %reduce-scatter.37.cloned.1.call-done = bf16[16,2304]{1,0:T(8,128)(2,1)} async-done(((bf16[256,2304]{1,0:T(8,128)(2,1)}), bf16[16,2304]{1,0:T(8,128)(2,1)}) %reduce-scatter.37.cloned.1.call-update) | async-done | bytes 73744 | tf_op jit(solution)/shard_map/reduce_scatter | solution.py:120
  412.0 23.5 %all_gather.38 = bf16[256,1152]{1,0:T(8,128)(2,1)S(1)} all-gather(bf16[16,1152]{1,0:T(8,128)(2,1)S(1)} %fusion.81), channel_id=1, replica_groups=mesh['dp'=16,'tp'=16] {'tp'}, dimensions={0}, use_global_device_ids=true | all-gather | bytes 626688 | tf_op jit(solution)/shard_map/all_gather | solution.py:129
  438.1 4.5 fusion.126
  442.7 47.4 %reduce-scatter.23.cloned.1.call-done = bf16[16,448]{1,0:T(8,128)(2,1)} async-done(((bf16[256,448]{1,0:T(8,128)(2,1)}), bf16[16,448]{1,0:T(8,128)(2,1)}) %reduce-scatter.23.cloned.1.call-update) | async-done | bytes 14352 | tf_op jit(solution)/shard_map/reduce_scatter | solution.py:130
  491.1 74.1 %all-reduce.1 = bf16[16,576]{1,0:T(8,128)(2,1)S(1)} all-reduce(bf16[16,576]{1,0:T(8,128)(2,1)S(1)} %convolution_convert_fusion.14), channel_id=6, replica_groups=mesh['dp'=16,'tp'=16] {'tp'}, use_global_device_ids=true, to_apply=%region_12.13.clone | all-reduce | flops 9216 | bytes 36864
  565.2 35.4 %psum.58 = f32[16]{0:T(128)S(1)} all-reduce(f32[16]{0:T(128)S(1)} %get-tuple-element.8), channel_id=1, replica_groups=mesh['dp'=16,'tp'=16] {'tp'}, use_global_device_ids=true, to_apply=%region_14.15 | all-reduce | flops 16 | bytes 128 | tf_op jit(solution)/shard_map/psum | solution.py:92
  606.0 3.9 fusion.36
  611.0 48.1 %all-gather.11.cloned.1.call-done = bf16[16,1,32768]{2,1,0:T(2,128)(2,1)} async-done(((bf16[1,1,32768]{2,1,0:T(2,128)(2,1)}), bf16[16,1,32768]{2,1,0:T(2,128)(2,1)}) %all-gather.11.cloned.1.call-update) | async-done | bytes 1048592 | tf_op jit(solution)/shard_map/all_gather | solution.py:103
  659.1 8.7 reduce.40
  669.2 44.7 %all_to_all.77 = bf16[16,16,2048]{2,0,1:T(8,128)(2,1)S(1)} all-to-all(bf16[16,16,2048]{2,0,1:T(8,128)(2,1)S(1)} %bitcast.249), channel_id=1, replica_groups=mesh['dp'=16,'tp'=16] {'dp'}, dimensions={1} | all-to-all | bytes 2097152 | tf_op jit(solution)/shard_map/all_to_all | solution.py:104
  715.5 50.9 %reduce-scatter.25.cloned.1.call-done = bf16[16,448]{1,0:T(8,128)(2,1)} async-done(((bf16[256,448]{1,0:T(8,128)(2,1)}), bf16[16,448]{1,0:T(8,128)(2,1)}) %reduce-scatter.25.cloned.1.call-update) | async-done | bytes 14352 | tf_op jit(solution)/shard_map/reduce_scatter | solution.py:105
  767.2 40.3 %psum.59 = f32[16]{0:T(128)S(1)} all-reduce(f32[16]{0:T(128)S(1)} %multiply_reduce_fusion.2), channel_id=1, replica_groups=mesh['dp'=16,'tp'=16] {'tp'}, use_global_device_ids=true, to_apply=%region_21.22 | all-reduce | flops 16 | bytes 128 | tf_op jit(solution)/shard_map/psum | solution.py:112
  808.2 18.3 all_gather.40
  833.3 72.1 %reduce-scatter.39.cloned.1.call-done = bf16[16,2304]{1,0:T(8,128)(2,1)} async-done(((bf16[256,2304]{1,0:T(8,128)(2,1)}), bf16[16,2304]{1,0:T(8,128)(2,1)}) %reduce-scatter.39.cloned.1.call-update) | async-done | bytes 73744 | tf_op jit(solution)/shard_map/reduce_scatter | solution.py:120
  906.3 23.6 %all_gather.41 = bf16[256,1152]{1,0:T(8,128)(2,1)S(1)} all-gather(bf16[16,1152]{1,0:T(8,128)(2,1)S(1)} %fusion.80), channel_id=1, replica_groups=mesh['dp'=16,'tp'=16] {'tp'}, dimensions={0}, use_global_device_ids=true | all-gather | bytes 626688 | tf_op jit(solution)/shard_map/all_gather | solution.py:129
  932.4 4.4 fusion.125
  936.8 47.5 %reduce-scatter.27.cloned.1.call-done = bf16[16,448]{1,0:T(8,128)(2,1)} async-done(((bf16[256,448]{1,0:T(8,128)(2,1)}), bf16[16,448]{1,0:T(8,128)(2,1)}) %reduce-scatter.27.cloned.1.call-update) | async-done | bytes 14352 | tf_op jit(solution)/shard_map/reduce_scatter | solution.py:130
  985.3 74.3 %all-reduce.2 = bf16[16,576]{1,0:T(8,128)(2,1)S(1)} all-reduce(bf16[16,576]{1,0:T(8,128)(2,1)S(1)} %convolution_convert_fusion.13), channel_id=10, replica_groups=mesh['dp'=16,'tp'=16] {'tp'}, use_global_device_ids=true, to_apply=%region_25.26.clone | all-reduce | flops 9216 | bytes 36864
  1059.7 35.4 %psum.60 = f32[16]{0:T(128)S(1)} all-reduce(f32[16]{0:T(128)S(1)} %get-tuple-element.6), channel_id=1, replica_groups=mesh['dp'=16,'tp'=16] {'tp'}, use_global_device_ids=true, to_apply=%region_27.28 | all-reduce | flops 16 | bytes 128 | tf_op jit(solution)/shard_map/psum | solution.py:92
  1105.5 48.1 %all-gather.13.cloned.1.call-done = bf16[16,1,32768]{2,1,0:T(2,128)(2,1)} async-done(((bf16[1,1,32768]{2,1,0:T(2,128)(2,1)}), bf16[16,1,32768]{2,1,0:T(2,128)(2,1)}) %all-gather.13.cloned.1.call-update) | async-done | bytes 1048592 | tf_op jit(solution)/shard_map/all_gather | solution.py:103
  1153.6 8.7 reduce.41
  1163.7 32.9 %all_to_all.78 = bf16[16,16,2048]{2,0,1:T(8,128)(2,1)S(1)} all-to-all(bf16[16,16,2048]{2,0,1:T(8,128)(2,1)S(1)} %bitcast.251), channel_id=1, replica_groups=mesh['dp'=16,'tp'=16] {'dp'}, dimensions={1} | all-to-all | bytes 2097152 | tf_op jit(solution)/shard_map/all_to_all | solution.py:104
  1198.1 51.0 %reduce-scatter.29.cloned.1.call-done = bf16[16,448]{1,0:T(8,128)(2,1)} async-done(((bf16[256,448]{1,0:T(8,128)(2,1)}), bf16[16,448]{1,0:T(8,128)(2,1)}) %reduce-scatter.29.cloned.1.call-update) | async-done | bytes 14352 | tf_op jit(solution)/shard_map/reduce_scatter | solution.py:105
  1249.9 40.3 %psum.61 = f32[16]{0:T(128)S(1)} all-reduce(f32[16]{0:T(128)S(1)} %multiply_reduce_fusion.1), channel_id=1, replica_groups=mesh['dp'=16,'tp'=16] {'tp'}, use_global_device_ids=true, to_apply=%region_34.35 | all-reduce | flops 16 | bytes 128 | tf_op jit(solution)/shard_map/psum | solution.py:112
  1291.1 18.3 all_gather.43
  1316.0 71.9 %reduce-scatter.41.cloned.1.call-done = bf16[16,2304]{1,0:T(8,128)(2,1)} async-done(((bf16[256,2304]{1,0:T(8,128)(2,1)}), bf16[16,2304]{1,0:T(8,128)(2,1)}) %reduce-scatter.41.cloned.1.call-update) | async-done | bytes 73744 | tf_op jit(solution)/shard_map/reduce_scatter | solution.py:120
  1388.9 23.5 %all_gather.44 = bf16[256,1152]{1,0:T(8,128)(2,1)S(1)} all-gather(bf16[16,1152]{1,0:T(8,128)(2,1)S(1)} %fusion.79), channel_id=1, replica_groups=mesh['dp'=16,'tp'=16] {'tp'}, dimensions={0}, use_global_device_ids=true | all-gather | bytes 626688 | tf_op jit(solution)/shard_map/all_gather | solution.py:129
  1415.0 4.4 fusion.124
  1419.5 47.5 %reduce-scatter.31.cloned.1.call-done = bf16[16,448]{1,0:T(8,128)(2,1)} async-done(((bf16[256,448]{1,0:T(8,128)(2,1)}), bf16[16,448]{1,0:T(8,128)(2,1)}) %reduce-scatter.31.cloned.1.call-update) | async-done | bytes 14352 | tf_op jit(solution)/shard_map/reduce_scatter | solution.py:130
  1468.0 74.1 %all-reduce.3 = bf16[16,576]{1,0:T(8,128)(2,1)S(1)} all-reduce(bf16[16,576]{1,0:T(8,128)(2,1)S(1)} %convolution_convert_fusion.12), channel_id=14, replica_groups=mesh['dp'=16,'tp'=16] {'tp'}, use_global_device_ids=true, to_apply=%region_38.39.clone | all-reduce | flops 9216 | bytes 36864
  1542.1 35.6 %psum.62 = f32[16]{0:T(128)S(1)} all-reduce(f32[16]{0:T(128)S(1)} %get-tuple-element.4), channel_id=1, replica_groups=mesh['dp'=16,'tp'=16] {'tp'}, use_global_device_ids=true, to_apply=%region_40.41 | all-reduce | flops 16 | bytes 128 | tf_op jit(solution)/shard_map/psum | solution.py:92
  1587.8 48.1 %all-gather.15.cloned.1.call-done = bf16[16,1,32768]{2,1,0:T(2,128)(2,1)} async-done(((bf16[1,1,32768]{2,1,0:T(2,128)(2,1)}), bf16[16,1,32768]{2,1,0:T(2,128)(2,1)}) %all-gather.15.cloned.1.call-update) | async-done | bytes 1048592 | tf_op jit(solution)/shard_map/all_gather | solution.py:103
  1636.0 7.7 reduce.42
  1643.8 33.0 %all_to_all.79 = bf16[16,16,2048]{2,0,1:T(8,128)(2,1)S(1)} all-to-all(bf16[16,16,2048]{2,0,1:T(8,128)(2,1)S(1)} %bitcast.252), channel_id=1, replica_groups=mesh['dp'=16,'tp'=16] {'dp'}, dimensions={1} | all-to-all | bytes 2097152 | tf_op jit(solution)/shard_map/all_to_all | solution.py:104
  1678.3 50.9 %reduce-scatter.33.cloned.1.call-done = bf16[16,448]{1,0:T(8,128)(2,1)} async-done(((bf16[256,448]{1,0:T(8,128)(2,1)}), bf16[16,448]{1,0:T(8,128)(2,1)}) %reduce-scatter.33.cloned.1.call-update) | async-done | bytes 14352 | tf_op jit(solution)/shard_map/reduce_scatter | solution.py:105
  1730.1 40.4 %psum.63 = f32[16]{0:T(128)S(1)} all-reduce(f32[16]{0:T(128)S(1)} %multiply_reduce_fusion), channel_id=1, replica_groups=mesh['dp'=16,'tp'=16] {'tp'}, use_global_device_ids=true, to_apply=%region_47.48 | all-reduce | flops 16 | bytes 128 | tf_op jit(solution)/shard_map/psum | solution.py:112
  1771.2 18.3 all_gather.46
  1794.3 71.9 %reduce-scatter.43.cloned.1.call-done = bf16[16,2304]{1,0:T(8,128)(2,1)} async-done(((bf16[256,2304]{1,0:T(8,128)(2,1)}), bf16[16,2304]{1,0:T(8,128)(2,1)}) %reduce-scatter.43.cloned.1.call-update) | async-done | bytes 73744 | tf_op jit(solution)/shard_map/reduce_scatter | solution.py:120
  1867.2 23.6 %all_gather.47 = bf16[256,1152]{1,0:T(8,128)(2,1)S(1)} all-gather(bf16[16,1152]{1,0:T(8,128)(2,1)S(1)} %fusion.78), channel_id=1, replica_groups=mesh['dp'=16,'tp'=16] {'tp'}, dimensions={0}, use_global_device_ids=true | all-gather | bytes 626688 | tf_op jit(solution)/shard_map/all_gather | solution.py:129
  1892.7 51.1 %reduce-scatter.35.cloned.1.call-done = bf16[16,448]{1,0:T(8,128)(2,1)} async-done(((bf16[256,448]{1,0:T(8,128)(2,1)}), bf16[16,448]{1,0:T(8,128)(2,1)}) %reduce-scatter.35.cloned.1.call-update) | async-done | bytes 14352 | tf_op jit(solution)/shard_map/reduce_scatter | solution.py:130
  (180 shorter events, 91.9 us)
Async XLA Ops:
  7.2 327.3 %copy-start = (bf16[2,448,1152]{2,1,0:T(8,128)(2,1)S(1)}, bf16[2,448,1152]{2,1,0:T(8,128)(2,1)}, u32[]{:S(2)}) copy-start(bf16[2,448,1152]{2,1,0:T(8,128)(2,1)} %param.20) | copy-start | bytes 6193156
  7.2 173.4 %all-gather.9.cloned.1.call-start = ((), (), s32[]{:S(2)}) async-start(), calls=%async_computation.24 | async-start | bytes 2228224 | tf_op jit(solution)/shard_map/all_gather | solution.py:103
  125.7 5.0 copy-start.1
  132.9 141.0 %reduce-scatter.21.cloned.1.call-start = ((), (), s32[]{:S(2)}) async-start(), calls=%async_computation.16 | async-start | bytes 278528 | tf_op jit(solution)/shard_map/reduce_scatter | solution.py:105
  188.3 33.1 %copy-start.12 = (bf16[2048,448]{0,1:T(8,128)(2,1)S(1)}, bf16[2048,448]{0,1:T(8,128)(2,1)}, u32[]{:S(2)}) copy-start(bf16[2048,448]{0,1:T(8,128)(2,1)} %param.18) | copy-start | bytes 5505028
  221.4 52.5 %copy-start.4 = (bf16[16,448]{1,0:T(8,128)(2,1)S(1)}, bf16[16,448]{1,0:T(8,128)(2,1)}, u32[]{:S(2)}) copy-start(bf16[16,448]{1,0:T(8,128)(2,1)} %param.11) | copy-start | bytes 43012
  221.4 93.7 %copy-start.10 = (f32[448]{0:T(512)S(1)}, f32[448]{0:T(512)}, u32[]{:S(2)}) copy-start(f32[448]{0:T(512)} %param.19) | copy-start | bytes 5380
  222.9 188.2 %reduce-scatter.37.cloned.1.call-start = ((), (), s32[]{:S(2)}) async-start(), calls=%async_computation.28 | async-start | bytes 1253376 | tf_op jit(solution)/shard_map/reduce_scatter | solution.py:120
  339.1 99.0 %copy-start.3 = (bf16[4,1,64,576]{3,2,1,0:T(8,128)(2,1)S(1)}, bf16[4,1,64,576]{3,2,1,0:T(8,128)(2,1)}, u32[]{:S(2)}) copy-start(bf16[4,1,64,576]{3,2,1,0:T(8,128)(2,1)} %param.12) | copy-start | bytes 884740
  339.1 150.9 %reduce-scatter.23.cloned.1.call-start = ((), (), s32[]{:S(2)}) async-start(), calls=%async_computation.17 | async-start | bytes 278528 | tf_op jit(solution)/shard_map/reduce_scatter | solution.py:130
  438.0 221.1 %all-gather.11.cloned.1.call-start = ((), (), s32[]{:S(2)}) async-start(), calls=%async_computation.25 | async-start | bytes 2228224 | tf_op jit(solution)/shard_map/all_gather | solution.py:103
  438.1 51.9 %copy-start.7 = (bf16[16,448]{1,0:T(8,128)(2,1)S(1)}, bf16[16,448]{1,0:T(8,128)(2,1)}, u32[]{:S(2)}) copy-start(bf16[16,448]{1,0:T(8,128)(2,1)} %reduce-scatter.21.cloned.1.call-done) | copy-start | bytes 43012
  438.1 52.8 %copy-start.2 = (bf16[448,576]{1,0:T(8,128)(2,1)S(1)}, bf16[448,576]{1,0:T(8,128)(2,1)}, u32[]{:S(2)}) copy-start(bf16[448,576]{1,0:T(8,128)(2,1)} %param.17) | copy-start | bytes 1548292
  438.1 52.8 %copy-start.9 = (f32[448]{0:T(512)S(1)}, f32[448]{0:T(512)}, u32[]{:S(2)}) copy-start(f32[448]{0:T(512)} %param.15) | copy-start | bytes 5380
  438.1 166.0 %copy-start.11 = (f32[512]{0:T(512)S(1)}, f32[512]{0:T(512)}, u32[]{:S(2)}) copy-start(f32[512]{0:T(512)} %param.16) | copy-start | bytes 6148
  610.9 155.4 %reduce-scatter.25.cloned.1.call-start = ((), (), s32[]{:S(2)}) async-start(), calls=%async_computation.18 | async-start | bytes 278528 | tf_op jit(solution)/shard_map/reduce_scatter | solution.py:105
  667.8 46.1 %copy-start.13 = (bf16[2048,448]{0,1:T(8,128)(2,1)S(1)}, bf16[2048,448]{0,1:T(8,128)(2,1)}, u32[]{:S(2)}) copy-start(bf16[2048,448]{0,1:T(8,128)(2,1)} %param.18) | copy-start | bytes 5505028
  715.4 189.9 %reduce-scatter.39.cloned.1.call-start = ((), (), s32[]{:S(2)}) async-start(), calls=%async_computation.29 | async-start | bytes 1253376 | tf_op jit(solution)/shard_map/reduce_scatter | solution.py:120
  833.2 151.1 %reduce-scatter.27.cloned.1.call-start = ((), (), s32[]{:S(2)}) async-start(), calls=%async_computation.19 | async-start | bytes 278528 | tf_op jit(solution)/shard_map/reduce_scatter | solution.py:130
  932.3 221.2 %all-gather.13.cloned.1.call-start = ((), (), s32[]{:S(2)}) async-start(), calls=%async_computation.26 | async-start | bytes 2228224 | tf_op jit(solution)/shard_map/all_gather | solution.py:103
  932.4 51.9 %copy-start.8 = (bf16[16,448]{1,0:T(8,128)(2,1)S(1)}, bf16[16,448]{1,0:T(8,128)(2,1)}, u32[]{:S(2)}) copy-start(bf16[16,448]{1,0:T(8,128)(2,1)} %reduce-scatter.25.cloned.1.call-done) | copy-start | bytes 43012
  1105.4 143.7 %reduce-scatter.29.cloned.1.call-start = ((), (), s32[]{:S(2)}) async-start(), calls=%async_computation.20 | async-start | bytes 278528 | tf_op jit(solution)/shard_map/reduce_scatter | solution.py:105
  1162.3 34.3 %copy-start.14 = (bf16[2048,448]{0,1:T(8,128)(2,1)S(1)}, bf16[2048,448]{0,1:T(8,128)(2,1)}, u32[]{:S(2)}) copy-start(bf16[2048,448]{0,1:T(8,128)(2,1)} %param.18) | copy-start | bytes 5505028
  1198.0 189.9 %reduce-scatter.41.cloned.1.call-start = ((), (), s32[]{:S(2)}) async-start(), calls=%async_computation.30 | async-start | bytes 1253376 | tf_op jit(solution)/shard_map/reduce_scatter | solution.py:120
  1316.0 150.9 %reduce-scatter.31.cloned.1.call-start = ((), (), s32[]{:S(2)}) async-start(), calls=%async_computation.21 | async-start | bytes 278528 | tf_op jit(solution)/shard_map/reduce_scatter | solution.py:130
  1414.9 221.0 %all-gather.15.cloned.1.call-start = ((), (), s32[]{:S(2)}) async-start(), calls=%async_computation.27 | async-start | bytes 2228224 | tf_op jit(solution)/shard_map/all_gather | solution.py:103
  1415.0 51.9 %copy-start.6 = (bf16[16,448]{1,0:T(8,128)(2,1)S(1)}, bf16[16,448]{1,0:T(8,128)(2,1)}, u32[]{:S(2)}) copy-start(bf16[16,448]{1,0:T(8,128)(2,1)} %reduce-scatter.29.cloned.1.call-done) | copy-start | bytes 43012
  1587.8 141.5 %reduce-scatter.33.cloned.1.call-start = ((), (), s32[]{:S(2)}) async-start(), calls=%async_computation.22 | async-start | bytes 278528 | tf_op jit(solution)/shard_map/reduce_scatter | solution.py:105
  1643.7 33.1 %copy-start.15 = (bf16[2048,448]{0,1:T(8,128)(2,1)S(1)}, bf16[2048,448]{0,1:T(8,128)(2,1)}, u32[]{:S(2)}) copy-start(bf16[2048,448]{0,1:T(8,128)(2,1)} %param.18) | copy-start | bytes 5505028
  1678.3 187.9 %reduce-scatter.43.cloned.1.call-start = ((), (), s32[]{:S(2)}) async-start(), calls=%async_computation.31 | async-start | bytes 1253376 | tf_op jit(solution)/shard_map/reduce_scatter | solution.py:120
  1791.8 98.9 %copy-start.16 = (bf16[1152,448]{0,1:T(8,128)(2,1)S(1)}, bf16[1152,448]{0,1:T(8,128)(2,1)}, u32[]{:S(2)}) copy-start(bf16[1152,448]{0,1:T(8,128)(2,1)} %param.21) | copy-start | bytes 3096580
  1794.3 149.6 %copy-start.5 = (bf16[16,448]{1,0:T(8,128)(2,1)S(1)}, bf16[16,448]{1,0:T(8,128)(2,1)}, u32[]{:S(2)}) copy-start(bf16[16,448]{1,0:T(8,128)(2,1)} %reduce-scatter.33.cloned.1.call-done) | copy-start | bytes 43012
  1794.3 149.6 %reduce-scatter.35.cloned.1.call-start = ((), (), s32[]{:S(2)}) async-start(), calls=%async_computation.23 | async-start | bytes 278528 | tf_op jit(solution)/shard_map/reduce_scatter | solution.py:130
Sparse Core Ops, SparseCore 0:
  133.0 47.4 all-gather.8
  223.0 50.8 reduce-scatter.20
  339.2 71.8 reduce-scatter.36
  438.2 51.8 reduce-scatter.22
  611.0 48.0 all-gather.10
  715.5 50.7 reduce-scatter.24
  833.3 71.9 reduce-scatter.38
  932.4 51.8 reduce-scatter.26
  1105.5 47.9 all-gather.12
  1198.2 50.8 reduce-scatter.28
  1316.1 71.8 reduce-scatter.40
  1415.1 51.8 reduce-scatter.30
  1587.9 48.0 all-gather.14
  1678.4 50.7 reduce-scatter.32
  1794.4 71.7 reduce-scatter.42
  1892.1 51.7 reduce-scatter.34
where the time goes:
time: 1970 us; the launch traced here: 1950 us
  blocking collectives  912 us (46%)
  waiting for transfers between devices  877 us (45%)
  other arithmetic  60.5 us (3%)
  matrix products  53.8 us (3%)
  local copies, waits for them, and re-layouts  26.9 us (1%)
  between operations  21.1 us (1%)
    unnamed x4, blocking collectives  292 us
    reduce_scatter x4, waiting for transfers between devices, body(): lax.psum_scatter(gate_and_up.reshape(every_row.shape[0] // tp_count * lax...  288 us
    reduce_scatter x4, waiting for transfers between devices, body(): lax.psum_scatter(jnp.dot(all_heads, w_out, preferred_element_type=jnp.flo...  204 us
    reduce_scatter x4, waiting for transfers between devices, body(): lax.psum_scatter(jnp.dot(hidden_all, w_down, preferred_element_type=jnp.f...  193 us
    all_gather x4, waiting for transfers between devices, body(): grouped = lax.all_gather(head_outputs, 'tp', axis=0, tiled=True)  192 us
    psum x4, blocking collectives, body(): mix_squares = lax.psum(jnp.sum(residual * residual, axis=1), 'tp')  161 us
    psum x4, blocking collectives, body(): all_squares = lax.psum(squares, 'tp')  147 us
    all_to_all x4, blocking collectives, body(): lax.all_to_all(grouped, 'dp', split_axis=1, concat_axis=0, tiled=True)  144 us
  transfers between devices with their start and end apart: 16, of which 16 were waited for; matrix products, arithmetic and copies ran while one was open for 1% of the time, Pallas kernels for 0%

commit v1 on v0

v1 whole, which is shorter than its diff:
```python
import functools

import jax
import jax.numpy as jnp
import numpy as np
from jax import lax
from jax.experimental import pallas as pl
from jax.experimental.pallas import tpu as pltpu
from jax.sharding import PartitionSpec as P

D = 7168
norm_eps = 1e-06
score_scale = 192.0 ** (-0.5)
MESH = pl.DeviceIdType.MESH
F32 = jnp.float32
BF16 = jnp.bfloat16
NT = (((1,), (1,)), ((), ()))


def layer_kernel(
    width,
    x_ref,
    q_ref,
    len_ref,
    ag_ref,
    kg_ref,
    mg_ref,
    freq_ref,
    kv_hbm,
    wl_hbm,
    wo_hbm,
    wgu_hbm,
    wd_hbm,
    out_ref,
    lat_out,
    kv,
    wl,
    wo,
    wgu,
    wd,
    scores,
    peak,
    total,
    old,
    states,
    resid,
    fresh,
    a_rows,
    a_send,
    a_recv,
    h_send,
    h_recv,
    heads,
    y_rows,
    y_send,
    y_recv,
    normed,
    g_send,
    g_recv,
    hidden,
    d_send,
    d_recv,
    load_sem,
    send_sem,
    recv_sem,
):
    n = x_ref.shape[0]
    steps, head_count, key_width = q_ref.shape
    lat = kg_ref.shape[1]
    ff = wd.shape[0]
    slots = kv.shape[0]
    chunks = load_sem.shape[0] - 4
    chunk = slots // chunks
    g = lax.axis_index("dp")
    t = lax.axis_index("tp")

    def load(src, dst, index):
        return pltpu.make_async_copy(src, dst, load_sem.at[index])

    load_wl = load(wl_hbm, wl, 0)
    load_wo = load(wo_hbm, wo, 1)
    load_wgu = load(wgu_hbm, wgu, 2)
    load_wd = load(wd_hbm, wd, 3)

    def load_kv(index):
        rows = pl.ds(pl.multiple_of(index * chunk, chunk), chunk)
        return load(kv_hbm.at[rows], kv.at[rows], 4 + index)

    load_wl.start()

    @pl.loop(0, chunks)
    def _(index):
        load_kv(index).start()

    load_wo.start()
    load_wgu.start()
    load_wd.start()

    barrier = pltpu.get_barrier_semaphore()

    @pl.loop(1, n)
    def _(i):
        pl.semaphore_signal(barrier, inc=1, device_id=(lax.rem(g + i, n), t), device_id_type=MESH)
        pl.semaphore_signal(barrier, inc=1, device_id=(g, lax.rem(t + i, n)), device_id_type=MESH)

    pl.semaphore_wait(barrier, 2 * (n - 1))

    def send_dp(phase, src, dst):
        @pl.loop(1, n)
        def _(i):
            peer = lax.rem(g + i, n)
            pltpu.make_async_remote_copy(
                src_ref=src(peer),
                dst_ref=dst(g),
                send_sem=send_sem.at[phase],
                recv_sem=recv_sem.at[phase],
                device_id=(peer, t),
                device_id_type=MESH,
            ).start()

    def send_tp(phase, src, dst):
        @pl.loop(1, n)
        def _(i):
            peer = lax.rem(t + i, n)
            pltpu.make_async_remote_copy(
                src_ref=src(peer),
                dst_ref=dst(t),
                send_sem=send_sem.at[phase],
                recv_sem=recv_sem.at[phase],
                device_id=(g, peer),
                device_id_type=MESH,
            ).start()

    def await_bytes(sem, ref):
        pltpu.make_async_copy(ref, ref, sem).wait()

    def rows_of(ref, index):
        return ref.at[pl.ds(pl.multiple_of(index * n, n), n)]

    def first_rows(ref):
        return ref.at[pl.ds(0, n * (n - 1))]

    def first_slots(ref):
        return ref.at[pl.ds(0, n - 1)]

    def send_latent():
        xs = states[...]
        scaled = (xs * ag_ref[...]).astype(BF16)
        a_rows[:, :key_width] = jnp.dot(scaled, wl[...], preferred_element_type=F32)
        squares = jnp.sum(xs * xs, axis=1, keepdims=True)
        a_rows[:, lat + 128 :] = jnp.broadcast_to(squares, (n, 128))
        for i in range(n):
            a_send[i] = a_rows[i : i + 1, :]
        a_recv[t] = a_send[t]
        send_tp(0, lambda peer: a_send.at[peer], lambda me: a_recv.at[me])

    a_rows[...] = jnp.zeros_like(a_rows)
    fresh[...] = jnp.zeros_like(fresh)
    states[...] = x_ref[...].astype(F32)
    load_wl.wait()
    send_latent()

    length = len_ref[0]
    queries = q_ref[...].reshape(steps * head_count, key_width)
    peak[...] = jnp.full_like(peak, -jnp.inf)

    @pl.loop(0, chunks)
    def _(index):
        load_kv(index).wait()
        rows = pl.ds(pl.multiple_of(index * chunk, chunk), chunk)
        part = lax.dot_general(queries, kv[rows], NT, preferred_element_type=F32) * score_scale
        place = lax.broadcasted_iota(jnp.int32, (1, chunk), 1) + index * chunk
        part = jnp.where(place < length, part, -jnp.inf)
        scores[:, rows] = part
        highest = peak[...]
        for k in range(0, chunk, 128):
            highest = jnp.maximum(highest, part[:, k : k + 128])
        peak[...] = highest

    top = jnp.max(peak[...], axis=1, keepdims=True)
    peak[...] = jnp.broadcast_to(top, peak.shape)
    total[...] = jnp.zeros_like(total)
    old[...] = jnp.zeros_like(old)

    @pl.loop(0, chunks)
    def _(index):
        rows = pl.ds(pl.multiple_of(index * chunk, chunk), chunk)
        weights = jnp.exp(scores[:, rows] - peak[:, :1])
        running = total[...]
        for k in range(0, chunk, 128):
            running = running + weights[:, k : k + 128]
        total[...] = running
        old[...] += jnp.dot(weights.astype(BF16), kv[rows, :lat], preferred_element_type=F32)

    total[...] = jnp.broadcast_to(jnp.sum(total[...], axis=1, keepdims=True), total.shape)
    load_wo.wait()
    load_wgu.wait()
    load_wd.wait()

    @pl.loop(0, steps)
    def _(s):
        await_bytes(recv_sem.at[0], first_slots(a_recv))
        await_bytes(send_sem.at[0], first_slots(a_send))
        raw = jnp.sum(a_recv[...], axis=0)
        inverse = lax.rsqrt(raw[:, lat + 128 : lat + 129] / width + norm_eps)
        raw = raw * inverse
        content = raw[:, :lat]
        spread = jnp.mean(content * content, axis=1, keepdims=True)
        content = content * lax.rsqrt(spread + norm_eps) * kg_ref[...]
        rope = raw[:, lat : lat + 128]
        half = (key_width - lat) // 2
        lane = lax.broadcasted_iota(jnp.int32, (1, 128), 1)
        angles = (length + s).astype(F32) * freq_ref[...]
        sine = jnp.sin(angles)
        turned = jnp.where(
            lane < half, -pltpu.roll(rope, 128 - half, 1), pltpu.roll(rope, half, 1)
        )
        rope = rope * jnp.cos(angles) + turned * sine
        latent = jnp.concatenate([content, rope], axis=1)[:, :key_width].astype(BF16)
        lat_out[s] = latent
        fresh[pl.ds(s, 1), :] = latent.astype(F32)

        keys = fresh[...].astype(BF16)
        recent = lax.dot_general(q_ref[s], keys, NT, preferred_element_type=F32) * score_scale
        column = lax.broadcasted_iota(jnp.int32, recent.shape, 1)
        recent = jnp.where(column <= s, recent, -jnp.inf)
        own = pl.ds(pl.multiple_of(s * head_count, head_count), head_count)
        top_old = peak[own, :1]
        highest = jnp.maximum(top_old, jnp.max(recent, axis=1, keepdims=True))
        keep = jnp.exp(top_old - highest)
        weight_new = jnp.exp(recent - highest)
        denominator = total[own, :1] * keep + jnp.sum(weight_new, axis=1, keepdims=True)
        prob_new = (weight_new / denominator).astype(BF16)
        joined = old[own, :] * (keep / denominator) + jnp.dot(
            prob_new, keys[:, :lat], preferred_element_type=F32
        )
        per = head_count // n
        for h in range(head_count):
            h_send[h // per, :, (h % per) * lat : (h % per + 1) * lat] = joined[h : h + 1, :]
        h_recv[g] = h_send[g]
        send_dp(1, lambda peer: h_send.at[peer], lambda me: h_recv.at[me])
        await_bytes(recv_sem.at[1], first_slots(h_recv))
        await_bytes(send_sem.at[1], first_slots(h_send))
        own_rows = pl.ds(pl.multiple_of(t * n, n), n)
        heads[own_rows, :] = h_recv[:, 0, :].astype(BF16)
        send_tp(2, lambda peer: rows_of(heads, t), lambda me: rows_of(heads, me))
        await_bytes(recv_sem.at[2], first_rows(heads))
        await_bytes(send_sem.at[2], first_rows(heads))

        attended = jnp.dot(heads[...], wo[...], preferred_element_type=F32)
        share = attended.shape[1]
        for k in range(0, share, 128):
            size = min(128, share - k)
            y_rows[k // 128, :, :size] = attended[:, k : k + size]
        for i in range(n):
            for k in range(0, share, 128):
                size = min(128, share - k)
                picked = y_rows[k // 128, pl.ds(i, n, stride=n), :]
                y_send[i, :, k : k + size] = picked[:, :size].astype(BF16)
        y_recv[g] = y_send[g]
        send_dp(3, lambda peer: y_send.at[peer], lambda me: y_recv.at[me])
        await_bytes(recv_sem.at[3], first_slots(y_recv))
        await_bytes(send_sem.at[3], first_slots(y_send))
        residual = states[...] + jnp.sum(y_recv[...].astype(F32), axis=0)
        resid[...] = residual

        own_rows = pl.ds(pl.multiple_of(g * n, n), n)
        normed[own_rows, :] = (residual * mg_ref[...]).astype(BF16)
        send_dp(4, lambda peer: rows_of(normed, g), lambda me: rows_of(normed, me))
        await_bytes(recv_sem.at[4], first_rows(normed))
        await_bytes(send_sem.at[4], first_rows(normed))
        unscaled = normed[...].astype(F32) / mg_ref[...]
        squares = jnp.sum(unscaled * unscaled, axis=1, keepdims=True)
        coarse = squares.astype(BF16).astype(F32)
        lane = lax.broadcasted_iota(jnp.int32, (n * n, 128), 1)
        g_send[:, 2 * ff :] = jnp.where(lane < 64, coarse, squares - coarse).astype(BF16)
        for k in range(2):
            g_send[:, k * ff : (k + 1) * ff] = jnp.dot(
                normed[...], wgu[k], preferred_element_type=F32
            ).astype(BF16)
        g_recv[t] = g_send[pl.ds(pl.multiple_of(t * n, n), n), :]
        send_tp(5, lambda peer: rows_of(g_send, peer), lambda me: g_recv.at[me])
        await_bytes(recv_sem.at[5], first_slots(g_recv))
        await_bytes(send_sem.at[5], first_rows(g_send))
        gate_up = jnp.sum(g_recv[...].astype(F32), axis=0)
        squares = jnp.sum(gate_up[:, 2 * ff :], axis=1, keepdims=True) / 64
        inverse = lax.rsqrt(squares / width + norm_eps)
        gate = gate_up[:, :ff] * inverse
        up = gate_up[:, ff : 2 * ff] * inverse
        own_rows = pl.ds(pl.multiple_of(t * n, n), n)
        hidden[own_rows, :] = (gate * jax.nn.sigmoid(gate) * up).astype(BF16)
        send_tp(6, lambda peer: rows_of(hidden, t), lambda me: rows_of(hidden, me))
        await_bytes(recv_sem.at[6], first_rows(hidden))
        await_bytes(send_sem.at[6], first_rows(hidden))

        d_send[...] = jnp.dot(hidden[...], wd[...], preferred_element_type=F32).astype(BF16)
        d_recv[g] = d_send[pl.ds(pl.multiple_of(g * n, n), n), :]
        send_dp(7, lambda peer: rows_of(d_send, peer), lambda me: d_recv.at[me])
        await_bytes(recv_sem.at[7], first_slots(d_recv))
        await_bytes(send_sem.at[7], first_rows(d_send))
        mixed = (resid[...] + jnp.sum(d_recv[...].astype(F32), axis=0)).astype(BF16)
        out_ref[s] = mixed
        states[...] = mixed.astype(F32)

        @pl.when(s < steps - 1)
        def _():
            send_latent()


def body(token_states, queries, kv_cache, lengths, attn_gain, kv_gain, w_latent, w_out, mlp_gain, w_gate_up, w_down):
    n, width = token_states.shape
    steps, _, head_count, key_width = queries.shape
    slots = kv_cache.shape[1]
    lat = kv_gain.shape[0]
    ff = w_down.shape[0]
    depth = w_out.shape[0]
    half = (key_width - lat) // 2
    frequency = np.zeros((1, 128), np.float32)
    frequency[0, : 2 * half] = np.tile(10000.0 ** (-np.arange(half) / half), 2)
    chunk = min(512, slots)
    rows = steps * head_count
    vmem = pl.BlockSpec(memory_space=pltpu.VMEM)
    hbm = pl.BlockSpec(memory_space=pl.ANY)
    mixed, latents = pl.pallas_call(
        functools.partial(layer_kernel, float(width * lax.axis_size("tp"))),
        out_shape=(
            jax.ShapeDtypeStruct((steps, n, width), BF16),
            jax.ShapeDtypeStruct((steps, 1, key_width), BF16),
        ),
        in_specs=[vmem, vmem, pl.BlockSpec(memory_space=pltpu.SMEM)] + [vmem] * 4 + [hbm] * 5,
        out_specs=(vmem, vmem),
        scratch_shapes=[
            pltpu.VMEM((slots, key_width), BF16),
            pltpu.VMEM(w_latent.shape, BF16),
            pltpu.VMEM(w_out.shape, BF16),
            pltpu.VMEM(w_gate_up.shape, BF16),
            pltpu.VMEM(w_down.shape, BF16),
            pltpu.VMEM((rows, slots), F32),
            pltpu.VMEM((rows, 128), F32),
            pltpu.VMEM((rows, 128), F32),
            pltpu.VMEM((rows, lat), F32),
            pltpu.VMEM((n, width), F32),
            pltpu.VMEM((n, width), F32),
            pltpu.VMEM((16, key_width), F32),
            pltpu.VMEM((n, lat + 256), F32),
            pltpu.VMEM((n, 1, lat + 256), F32),
            pltpu.VMEM((n, 1, lat + 256), F32),
            pltpu.VMEM((n, 1, depth), F32),
            pltpu.VMEM((n, 1, depth), F32),
            pltpu.VMEM((n * n, depth), BF16),
            pltpu.VMEM((-(-width // 128), n * n, 128), F32),
            pltpu.VMEM((n, n, width), BF16),
            pltpu.VMEM((n, n, width), BF16),
            pltpu.VMEM((n * n, width), BF16),
            pltpu.VMEM((n * n, 2 * ff + 128), BF16),
            pltpu.VMEM((n, n, 2 * ff + 128), BF16),
            pltpu.VMEM((n * n, ff), BF16),
            pltpu.VMEM((n * n, width), BF16),
            pltpu.VMEM((n, n, width), BF16),
            pltpu.SemaphoreType.DMA((4 + slots // chunk,)),
            pltpu.SemaphoreType.DMA((8,)),
            pltpu.SemaphoreType.DMA((8,)),
        ],
        compiler_params=pltpu.CompilerParams(
            collective_id=0, has_side_effects=True, vmem_limit_bytes=48 * 1024 * 1024
        ),
        name="decode_layer",
    )(
        token_states,
        queries.reshape(steps, head_count, key_width),
        lengths,
        attn_gain.reshape(1, -1),
        kv_gain.reshape(1, -1),
        mlp_gain.reshape(1, -1),
        jnp.asarray(frequency),
        kv_cache.reshape(slots, key_width),
        w_latent,
        w_out,
        w_gate_up,
        w_down,
    )
    return mixed, latents


def solution(mesh):
    placed = (
        P("dp", "tp"),
        P(None, ("dp", "tp"), None, None),
        P(("dp", "tp"), None, None),
        P(("dp", "tp")),
        P("tp"),
        P(),
        P("tp", None),
        P("dp", "tp"),
        P("tp"),
        P(None, "tp", "dp"),
        P("dp", "tp"),
    )
    return jax.shard_map(
        body,
        mesh=mesh,
        in_specs=placed,
        out_specs=(P(None, "dp", "tp"), P(None, ("dp", "tp"), None)),
        check_vma=False,
    )
```

time: 1970 us -> 372 us (0.19)
  blocking collectives: 912 us -> 0 us
  waiting for transfers between devices: 877 us -> 0 us
  Pallas kernels: 0 us -> 354 us
  other arithmetic: 60.5 us -> 0 us
  matrix products: 53.8 us -> 0 us
    reduce_scatter x12 -> x0, waiting for transfers between devices: 685 us -> none  [the longest x4 288 us: body(): lax.psum_scatter(gate_and_up.reshape(every_row.shape[0] // tp_count * lax...]
    pallas_call x0 -> x1, Pallas kernels: none -> 354 us  [body(): pl.pallas_call(functools.partial(layer_kernel, float(width * lax.axis_siz...]
    psum x8 -> x0, blocking collectives: 308 us -> none  [the longest x4 161 us: body(): mix_squares = lax.psum(jnp.sum(residual * residual, axis=1), 'tp')]
    unnamed x4 -> x0, blocking collectives: 292 us -> none
    all_gather x4 -> x0, waiting for transfers between devices: 192 us -> none  [body(): grouped = lax.all_gather(head_outputs, 'tp', axis=0, tiled=True)]
    all_gather x8 -> x0, blocking collectives: 168 us -> none  [the longest x4 94.2 us: body(): hidden_all = lax.all_gather(hidden, 'tp', axis=0, tiled=True)]
    all_to_all x4 -> x0, blocking collectives: 144 us -> none  [body(): lax.all_to_all(grouped, 'dp', split_axis=1, concat_axis=0, tiled=True)]
    dot_general x31 -> x0, matrix products: 53.8 us -> none  [the longest x4 17 us: attend_local(): jnp.einsum('uhk,ulk->uhl', query_block, kv_cache, preferred_element_type=...]
  transfers between devices with their start and end apart: 16 -> 0, of which waited for: 16 -> 0; matrix products, arithmetic and copies ran while one was open for 1% -> 0% of each run, Pallas kernels for 0% -> 0%
where the time goes in v1:
time: 372 us; the launch traced here: 371 us
  Pallas kernels  354 us (95%)
  local copies, waits for them, and re-layouts  15.3 us (4%)
    pallas_call x1, Pallas kernels, body(): pl.pallas_call(functools.partial(layer_kernel, float(width * lax.axis_siz...  354 us
    unnamed x22, local copies, waits for them, and re-layouts  14.7 us

profile of v1, /device:TPU:32, one launch (start us, length us, event | category | flops | bytes accessed | tf_op | source)
XLA Modules:
  0.0 370.9 jit_solution(16624900526452242409)
XLA Ops:
  0.6 0.0 copy-start.8
  1.4 1.7 copy.16.wd_hbm
  3.2 0.0 copy-done.8
  3.2 2.5 copy.15.wo_hbm
  5.6 0.0 copy-start
  5.7 0.0 copy-start.3
  5.7 0.0 copy-start.4
  5.7 0.0 copy-start.5
  5.7 0.0 copy-start.6
  5.7 0.0 copy-start.7
  5.7 7.8 %copy.14 = bf16[1,4096,576]{2,1,0:T(8,128)(2,1)} copy(bf16[1,4096,576]{1,2,0:T(8,128)(2,1)} %param.14) | data formatting | bytes 9437184 | tf_op args[2]
  13.4 0.0 copy-done
  13.5 0.0 copy-done.3
  13.5 0.0 copy-done.4
  13.5 0.0 copy-done.5
  13.5 0.0 copy-done.6
  13.5 0.0 copy-done.7
  13.5 0.0 copy-start.1
  13.5 1.1 copy-done.1
  14.6 0.0 copy-start.2
  14.6 1.0 copy-done.2
  15.5 354.1 %decode_layer.1 = (bf16[4,16,448]{2,1,0:T(8,128)(2,1)S(1)}, bf16[4,1,576]{2,1,0:T(2,128)(2,1)S(1)}) custom-call(bf16[16,448]{1,0:T(8,128)(2,1)S(1)} %copy-done.3, bf16[4,64,576]{2,1,0:T(8,128)(2,1)S(1)} %bitcast.5, s32[1]{0:T(128)S(6)} %copy.19.len_ref, f32[1,448]{1,0:T(1,128)S(1)} %bitcast.6, f32[1,512]{1,0:T(1,128)S(1)} %bitcast.7, f32[1,448]{1,0:T(1,128)S(1)} %bitcast.8, ...), custom_call_target="tpu_custom_call" | custom-call | tf_op jit(solution)/shard_map/decode_layer/pallas_call | solution.py:324
  369.7 0.6 copy.17
  370.3 0.6 copy.20
Async XLA Ops:
  0.6 2.5 copy-start.8
  5.6 7.8 %copy-start = (bf16[2,448,1152]{2,1,0:T(8,128)(2,1)S(1)}, bf16[2,448,1152]{2,1,0:T(8,128)(2,1)}, u32[]{:S(2)}) copy-start(bf16[2,448,1152]{2,1,0:T(8,128)(2,1)} %wgu_hbm.1) | copy-start | bytes 6193156
  5.7 7.8 %copy-start.3 = (bf16[16,448]{1,0:T(8,128)(2,1)S(1)}, bf16[16,448]{1,0:T(8,128)(2,1)}, u32[]{:S(2)}) copy-start(bf16[16,448]{1,0:T(8,128)(2,1)} %x_ref.1) | copy-start | bytes 43012
  5.7 7.8 %copy-start.4 = (f32[448]{0:T(512)S(1)}, f32[448]{0:T(512)}, u32[]{:S(2)}) copy-start(f32[448]{0:T(512)} %param.16) | copy-start | bytes 5380
  5.7 7.8 %copy-start.5 = (f32[512]{0:T(512)S(1)}, f32[512]{0:T(512)}, u32[]{:S(2)}) copy-start(f32[512]{0:T(512)} %param.17) | copy-start | bytes 6148
  5.7 7.8 %copy-start.6 = (f32[448]{0:T(512)S(1)}, f32[448]{0:T(512)}, u32[]{:S(2)}) copy-start(f32[448]{0:T(512)} %param.20) | copy-start | bytes 5380
  5.7 7.8 %copy-start.7 = (f32[1,128]{1,0:T(1,128)S(1)}, f32[1,128]{1,0:T(1,128)}, u32[]{:S(2)}) copy-start(f32[1,128]{1,0:T(1,128)} %constant.2.clone.freq_ref) | copy-start | bytes 1540
  13.5 1.1 copy-start.1
  14.6 1.0 copy-start.2

commit v2 on v1

v2 whole, which is shorter than its diff:
```python
import functools

import jax
import jax.numpy as jnp
import numpy as np
from jax import lax
from jax.experimental import pallas as pl
from jax.experimental.pallas import tpu as pltpu
from jax.sharding import PartitionSpec as P

D = 7168
norm_eps = 1e-06
score_scale = 192.0 ** (-0.5)
MESH = pl.DeviceIdType.MESH
F32 = jnp.float32
BF16 = jnp.bfloat16
NT = (((1,), (1,)), ((), ()))


def layer_kernel(
    width,
    x_hbm,
    q_hbm,
    len_ref,
    ag_hbm,
    kg_hbm,
    mg_hbm,
    freq_hbm,
    kv_hbm,
    wl_hbm,
    wo_hbm,
    wgu_hbm,
    wd_hbm,
    out_ref,
    lat_out,
    x_ref,
    q_ref,
    ag_ref,
    kg_ref,
    mg_ref,
    freq_ref,
    kv,
    wl,
    wo,
    wgu,
    wd,
    scores,
    peak,
    total,
    old,
    states,
    resid,
    fresh,
    a_rows,
    a_send,
    a_recv,
    o_send,
    o_recv,
    old_heads,
    b_send,
    b_recv,
    l_all,
    latents,
    heads,
    y_rows,
    y_send,
    y_recv,
    normed,
    gate_send,
    gate_recv,
    gate_mid,
    gate_last,
    up_send,
    up_recv,
    up_mid,
    up_last,
    hidden,
    d_send,
    d_recv,
    load_sem,
    swap_send,
    swap_recv,
    send_sem,
    recv_sem,
    o_sem,
    o_sent,
    p_sem,
    p_sent,
):
    nt = x_ref.shape[0]
    nz = nt // 2
    side = gate_recv.shape[0]
    steps, head_count, key_width = q_ref.shape
    lat = kg_ref.shape[1]
    ff = wd.shape[2]
    share = wd.shape[1]
    slots = kv.shape[1]
    per = head_count // nz
    half_per = per // 2
    chunks = load_sem.shape[0] - 10
    chunk = slots // chunks
    g = lax.axis_index("dp")
    z = g // 2
    c = lax.rem(g, 2)
    t = lax.axis_index("tp")
    xx = t // side
    yy = lax.rem(t, side)
    sibling = (z * 2 + 1 - c, t)

    def z_peer(i):
        peer = lax.rem(z + i, nz)
        return peer, (peer * 2 + c, t)

    def t_peer(i):
        peer = lax.rem(t + i, nt)
        return peer, (g, peer)

    def x_peer(i):
        peer = lax.rem(xx + i, side)
        return peer, (g, peer * side + yy)

    def y_peer(i):
        peer = lax.rem(yy + i, side)
        return peer, (g, xx * side + peer)

    def load(source, target, index):
        return pltpu.make_async_copy(source, target, load_sem.at[index])

    loads = [
        load(x_hbm, x_ref, 0),
        load(ag_hbm, ag_ref, 1),
        load(wl_hbm, wl, 2),
        load(q_hbm, q_ref, 3),
        load(kg_hbm, kg_ref, 4),
        load(freq_hbm, freq_ref, 5),
        load(mg_hbm, mg_ref, 6),
    ]
    for one in loads:
        one.start()

    def load_kv(index):
        place = pl.ds(pl.multiple_of(index * chunk, chunk), chunk)
        return load(kv_hbm.at[:, place], kv.at[:, place], 10 + index)

    @pl.loop(0, chunks)
    def _(index):
        load_kv(index).start()

    own_weights = [
        load(wo_hbm, wo.at[c], 7),
        load(wgu_hbm, wgu.at[c], 8),
        load(wd_hbm, wd.at[c], 9),
    ]
    for one in own_weights:
        one.start()

    barrier = pltpu.get_barrier_semaphore()

    @pl.loop(1, nz)
    def _(i):
        pl.semaphore_signal(barrier, inc=1, device_id=z_peer(i)[1], device_id_type=MESH)

    @pl.loop(1, nt)
    def _(i):
        pl.semaphore_signal(barrier, inc=1, device_id=t_peer(i)[1], device_id_type=MESH)

    pl.semaphore_signal(barrier, inc=1, device_id=sibling, device_id_type=MESH)
    pl.semaphore_wait(barrier, nz + nt - 1)

    def push(source, target, sent, landed, device):
        return pltpu.make_async_remote_copy(
            src_ref=source,
            dst_ref=target,
            send_sem=sent,
            recv_sem=landed,
            device_id=device,
            device_id_type=MESH,
        )

    swaps = [
        push(source, target.at[c], swap_send.at[k], swap_recv.at[k], sibling)
        for k, (source, target) in enumerate(((wo_hbm, wo), (wgu_hbm, wgu), (wd_hbm, wd)))
    ]

    def send(phase, peer_of, count, source, target):
        @pl.loop(1, count)
        def _(i):
            peer, device = peer_of(i)
            push(source(peer), target, send_sem.at[phase], recv_sem.at[phase], device).start()

    def await_bytes(sem, ref):
        pltpu.make_async_copy(ref, ref, sem).wait()

    def block(ref, index):
        return ref.at[pl.ds(pl.multiple_of(index * nt, nt), nt)]

    def first(ref, count):
        return ref.at[pl.ds(0, count)]

    def landed(phase, ref):
        await_bytes(recv_sem.at[phase], ref)

    def sent(phase, ref):
        await_bytes(send_sem.at[phase], ref)

    def send_latent():
        xs = states[...]
        scaled = (xs * ag_ref[...]).astype(BF16)
        a_rows[:, :key_width] = jnp.dot(scaled, wl[...], preferred_element_type=F32)
        squares = jnp.sum(xs * xs, axis=1, keepdims=True)
        a_rows[:, lat + 128 :] = jnp.broadcast_to(squares, (nt, 128))
        for i in range(nt):
            a_send[i] = a_rows[i : i + 1, :]
        a_recv[t] = a_send[t]
        send(0, t_peer, nt, lambda peer: a_send.at[peer], a_recv.at[t])

    a_rows[...] = jnp.zeros_like(a_rows)
    fresh[...] = jnp.zeros_like(fresh)
    latents[...] = jnp.zeros_like(latents)
    for one in loads[:3]:
        one.wait()
    states[...] = x_ref[...].astype(F32)
    send_latent()
    for one in swaps:
        one.start()

    length = len_ref[0]
    for one in loads[3:]:
        one.wait()
    queries = q_ref[...].reshape(steps * head_count, key_width)
    peak[...] = jnp.full_like(peak, -jnp.inf)

    @pl.loop(0, chunks)
    def _(index):
        load_kv(index).wait()
        place = pl.ds(pl.multiple_of(index * chunk, chunk), chunk)
        part = jnp.dot(queries, kv[:, place], preferred_element_type=F32) * score_scale
        column = lax.broadcasted_iota(jnp.int32, (1, chunk), 1) + index * chunk
        part = jnp.where(column < length, part, -jnp.inf)
        scores[:, place] = part
        highest = peak[...]
        for k in range(0, chunk, 128):
            highest = jnp.maximum(highest, part[:, k : k + 128])
        peak[...] = highest

    top = jnp.max(peak[...], axis=1, keepdims=True)
    peak[...] = jnp.broadcast_to(top, peak.shape)
    total[...] = jnp.zeros_like(total)
    old[...] = jnp.zeros_like(old)

    @pl.loop(0, chunks)
    def _(index):
        place = pl.ds(pl.multiple_of(index * chunk, chunk), chunk)
        weights = jnp.exp(scores[:, place] - peak[:, :1])
        running = total[...]
        for k in range(0, chunk, 128):
            running = running + weights[:, k : k + 128]
        total[...] = running
        old[...] += lax.dot_general(
            weights.astype(BF16), kv[:lat, place], NT, preferred_element_type=F32
        )

    total[...] = jnp.broadcast_to(jnp.sum(total[...], axis=1, keepdims=True), total.shape)

    @pl.loop(0, steps)
    def _(s):
        rows = pl.ds(pl.multiple_of(s * head_count, head_count), head_count)
        whole = old[rows, :] / total[rows, :1]
        for h in range(head_count):
            o_send[s, h] = whole[h : h + 1, :]
        mine = pl.ds(z * per, per)
        o_recv[s, :, z] = o_send[s, mine]

        @pl.loop(1, nz)
        def _(i):
            peer, device = z_peer(i)
            theirs = pl.ds(peer * per, per)
            push(
                o_send.at[s, theirs], o_recv.at[s, :, z], o_sent.at[s], o_sem.at[s], device
            ).start()

    def spread_old(s):
        await_bytes(o_sem.at[s], o_send.at[s, pl.ds(0, per * (nz - 1))])
        await_bytes(o_sent.at[s], o_send.at[s, pl.ds(0, per * (nz - 1))])
        for h in range(half_per):
            pair = [o_recv[s, k * half_per + h, :, 0, :] for k in range(2)]
            old_heads[s, t, :, h * lat : (h + 1) * lat] = jnp.concatenate(pair, axis=0).astype(BF16)

        @pl.loop(1, nt)
        def _(i):
            part = old_heads.at[s, t]
            push(part, part, p_sent.at[s], p_sem.at[s], t_peer(i)[1]).start()

    spread_old(0)
    for one in own_weights:
        one.wait()
    for one in swaps:
        one.wait()

    @pl.loop(0, steps)
    def _(s):
        landed(0, first(a_recv, nt - 1))
        sent(0, first(a_send, nt - 1))
        raw = jnp.sum(a_recv[...], axis=0)
        inverse = lax.rsqrt(raw[:, lat + 128 : lat + 129] / width + norm_eps)
        raw = raw * inverse
        content = raw[:, :lat]
        spread = jnp.mean(content * content, axis=1, keepdims=True)
        content = content * lax.rsqrt(spread + norm_eps) * kg_ref[...]
        rope = raw[:, lat : lat + 128]
        half = (key_width - lat) // 2
        lane = lax.broadcasted_iota(jnp.int32, (1, 128), 1)
        angles = (length + s).astype(F32) * freq_ref[...]
        sine = jnp.sin(angles)
        turned = jnp.where(
            lane < half, -pltpu.roll(rope, 128 - half, 1), pltpu.roll(rope, half, 1)
        )
        rope = rope * jnp.cos(angles) + turned * sine
        latent = jnp.concatenate([content, rope], axis=1)[:, :key_width].astype(BF16)
        lat_out[s] = latent
        fresh[pl.ds(s, 1), :] = latent.astype(F32)

        keys = fresh[...].astype(BF16)
        recent = lax.dot_general(q_ref[s], keys, NT, preferred_element_type=F32) * score_scale
        column = lax.broadcasted_iota(jnp.int32, recent.shape, 1)
        recent = jnp.where(column <= s, recent, -jnp.inf)
        own = pl.ds(pl.multiple_of(s * head_count, head_count), head_count)
        top_old = peak[own, :1]
        highest = jnp.maximum(top_old, jnp.max(recent, axis=1, keepdims=True))
        weight_old = total[own, :1] * jnp.exp(top_old - highest)
        weight_new = jnp.exp(recent - highest)
        denominator = weight_old + jnp.sum(weight_new, axis=1, keepdims=True)
        share_new = (weight_new / denominator).astype(BF16).astype(F32)
        column = lax.broadcasted_iota(jnp.int32, (head_count, 128), 1)
        table = jnp.where(column == 0, weight_old / denominator, 0.0)
        for j in range(steps):
            table = jnp.where(column == j + 1, share_new[:, j : j + 1], table)
        table = jnp.concatenate([table, jnp.zeros((128 - head_count, 128), F32)], axis=0).T
        b_send[0, :, :lat] = latent[:, :lat].astype(F32)
        for k in range(steps + 1):
            b_send[0, :, lat + k * 128 : lat + (k + 1) * 128] = table[k : k + 1, :]
        b_recv[z] = b_send[0]
        send(1, z_peer, nz, lambda peer: b_send.at[0], b_recv.at[z])
        landed(1, first(b_recv, nz - 1))
        sent(1, first(b_recv, nz - 1))
        news = b_recv[:, 0, :]
        lane = lax.broadcasted_iota(jnp.int32, (nz, 128), 1)
        coarse = jnp.zeros((nz, 128), F32)
        for k in range(steps + 1):
            moved = pltpu.roll(
                news[:, lat + k * 128 : lat + (k + 1) * 128],
                lax.rem(k * per - z * per + 128, 128),
                1,
            )
            coarse = jnp.where((lane >= k * per) & (lane < (k + 1) * per), moved, coarse)
        fine = coarse - coarse.astype(BF16).astype(F32)
        upper = jnp.concatenate([news[:, : lat // 2], coarse], axis=1)
        lower = jnp.concatenate([news[:, lat // 2 : lat], fine], axis=1)
        l_all[t] = jnp.concatenate([upper, lower], axis=0).astype(BF16)
        send(2, t_peer, nt, lambda peer: l_all.at[t], l_all.at[t])
        await_bytes(p_sem.at[s], old_heads.at[s, pl.ds(0, nt - 1)])
        await_bytes(p_sent.at[s], old_heads.at[s, pl.ds(0, nt - 1)])
        landed(2, first(l_all, nt - 1))
        sent(2, first(l_all, nt - 1))

        news = l_all[...].astype(F32)
        upper = news[:, :nz, :].reshape(nt * nz, -1)
        lower = news[:, nz:, :].reshape(nt * nz, -1)
        latents[s] = jnp.concatenate([upper[:, : lat // 2], lower[:, : lat // 2]], axis=1)
        table = upper[:, lat // 2 :] + lower[:, lat // 2 :]
        for h in range(half_per):
            pair = old_heads[s, :, :, h * lat : (h + 1) * lat].astype(F32)
            for k in range(2):
                number = k * half_per + h
                joined = pair[:, k * nz : (k + 1) * nz, :].reshape(nt * nz, lat)
                joined = joined * table[:, number : number + 1]
                for j in range(steps):
                    at = (j + 1) * per + number
                    joined = joined + latents[j] * table[:, at : at + 1]
                heads[k, :, h * lat : (h + 1) * lat] = joined.astype(BF16)

        attended = sum(
            lax.dot_general(heads[k], wo[k], NT, preferred_element_type=F32) for k in range(2)
        )
        for k in range(0, share, 128):
            size = min(128, share - k)
            y_rows[k // 128, :, :size] = attended[:, k : k + size]
        for i in range(nz):
            for k in range(0, share, 128):
                size = min(128, share - k)
                picked = y_rows[k // 128, pl.ds(i, nt, stride=nz), :]
                y_send[i, :, k : k + size] = picked[:, :size].astype(BF16)
        y_recv[z] = y_send[z]
        send(3, z_peer, nz, lambda peer: y_send.at[peer], y_recv.at[z])

        @pl.when(s < steps - 1)
        def _():
            spread_old(s + 1)

        landed(3, first(y_recv, nz - 1))
        sent(3, first(y_send, nz - 1))
        residual = states[...] + jnp.sum(y_recv[...].astype(F32), axis=0)
        resid[...] = residual

        block(normed, z)[...] = (residual * mg_ref[...]).astype(BF16)
        send(4, z_peer, nz, lambda peer: block(normed, z), block(normed, z))
        landed(4, first(normed, nt * (nz - 1)))
        sent(4, first(normed, nt * (nz - 1)))

        rows = normed[...]
        for k in range(2):
            gate = jnp.dot(rows, wgu[k, 0], preferred_element_type=F32).astype(BF16)
            for i in range(nz):
                place = 2 * i + k
                gate_send[place // side, place % side, :, :ff] = gate[i * nt : (i + 1) * nt, :]
        unscaled = rows.astype(F32) / mg_ref[...]
        squares = jnp.sum(unscaled * unscaled, axis=1, keepdims=True)
        coarse = squares.astype(BF16).astype(F32)
        lane = lax.broadcasted_iota(jnp.int32, (nt * nz, 128), 1)
        parts = jnp.where(lane < 64, coarse, squares - coarse).astype(BF16)
        for i in range(nt):
            here = i // 2 * nt
            gate_send[i // side, i % side, :, ff:] = parts[here : here + nt, :]
        gate_recv[xx] = gate_send[xx]
        send(5, x_peer, side, lambda peer: gate_send.at[peer], gate_recv.at[xx])
        for k in range(2):
            up = jnp.dot(rows, wgu[k, 1], preferred_element_type=F32).astype(BF16)
            for i in range(nz):
                place = 2 * i + k
                up_send[place % side, place // side] = up[i * nt : (i + 1) * nt, :]
        up_recv[yy] = up_send[yy]
        send(6, y_peer, side, lambda peer: up_send.at[peer], up_recv.at[yy])
        landed(5, first(gate_recv, side - 1))
        for i in range(side):
            gate_mid[i] = jnp.sum(gate_recv[:, i].astype(F32), axis=0).astype(BF16)
        gate_last[yy] = gate_mid[yy]
        send(7, y_peer, side, lambda peer: gate_mid.at[peer], gate_last.at[yy])
        landed(6, first(up_recv, side - 1))
        for i in range(side):
            up_mid[i] = jnp.sum(up_recv[:, i].astype(F32), axis=0).astype(BF16)
        up_last[xx] = up_mid[xx]
        send(8, x_peer, side, lambda peer: up_mid.at[peer], up_last.at[xx])
        sent(5, first(gate_send, side - 1))
        sent(6, first(up_send, side - 1))
        landed(7, first(gate_last, side - 1))
        gate = jnp.sum(gate_last[...].astype(F32), axis=0)
        squares = jnp.sum(gate[:, ff:], axis=1, keepdims=True) / 64
        inverse = lax.rsqrt(squares / width + norm_eps)
        gate = gate[:, :ff] * inverse
        gate = gate * jax.nn.sigmoid(gate) * inverse
        landed(8, first(up_last, side - 1))
        up = jnp.sum(up_last[...].astype(F32), axis=0)
        place = lax.rem(t, 2) * nz + t // 2
        block(hidden, place)[...] = (gate * up).astype(BF16)
        send(9, t_peer, nt, lambda peer: block(hidden, place), block(hidden, place))
        sent(7, first(gate_mid, side - 1))
        sent(8, first(up_mid, side - 1))
        landed(9, first(hidden, nt * (nt - 1)))
        sent(9, first(hidden, nt * (nt - 1)))

        down = sum(
            lax.dot_general(
                hidden[k * nz * nt : (k + 1) * nz * nt, :], wd[k], NT, preferred_element_type=F32
            )
            for k in range(2)
        )
        d_send[...] = down.astype(BF16)
        d_recv[z] = block(d_send, z)[...]
        send(10, z_peer, nz, lambda peer: block(d_send, peer), d_recv.at[z])
        landed(10, first(d_recv, nz - 1))
        sent(10, first(d_recv, nz - 1))
        mixed = (resid[...] + jnp.sum(d_recv[...].astype(F32), axis=0)).astype(BF16)
        out_ref[s] = mixed
        states[...] = mixed.astype(F32)

        @pl.when(s < steps - 1)
        def _():
            send_latent()


def body(token_states, queries, kv_cache, lengths, attn_gain, kv_gain, w_latent, w_out, mlp_gain, w_gate_up, w_down):
    nt, width = token_states.shape
    nz = nt // 2
    side = int(round(nt**0.5))
    steps, _, head_count, key_width = queries.shape
    slots = kv_cache.shape[1]
    lat = kv_gain.shape[0]
    ff = w_down.shape[0]
    depth = w_out.shape[0]
    per = head_count // nz
    half = (key_width - lat) // 2
    frequency = np.zeros((1, 128), np.float32)
    frequency[0, : 2 * half] = np.tile(10000.0 ** (-np.arange(half) / half), 2)
    chunk = min(512, slots)
    rows = steps * head_count
    vmem = pl.BlockSpec(memory_space=pltpu.VMEM)
    hbm = pl.BlockSpec(memory_space=pl.ANY)
    news = lat + (steps + 1) * 128
    block = lat // 2 + 128
    mixed, latents = pl.pallas_call(
        functools.partial(layer_kernel, float(width * lax.axis_size("tp"))),
        out_shape=(
            jax.ShapeDtypeStruct((steps, nt, width), BF16),
            jax.ShapeDtypeStruct((steps, 1, key_width), BF16),
        ),
        in_specs=[hbm, hbm, pl.BlockSpec(memory_space=pltpu.SMEM)] + [hbm] * 9,
        out_specs=(vmem, vmem),
        scratch_shapes=[
            pltpu.VMEM((nt, width), BF16),
            pltpu.VMEM((steps, head_count, key_width), BF16),
            pltpu.VMEM((1, width), F32),
            pltpu.VMEM((1, lat), F32),
            pltpu.VMEM((1, width), F32),
            pltpu.VMEM((1, 128), F32),
            pltpu.VMEM((key_width, slots), BF16),
            pltpu.VMEM(w_latent.shape, BF16),
            pltpu.VMEM((2, width, depth), BF16),
            pltpu.VMEM((2,) + w_gate_up.shape, BF16),
            pltpu.VMEM((2, width, ff), BF16),
            pltpu.VMEM((rows, slots), F32),
            pltpu.VMEM((rows, 128), F32),
            pltpu.VMEM((rows, 128), F32),
            pltpu.VMEM((rows, lat), F32),
            pltpu.VMEM((nt, width), F32),
            pltpu.VMEM((nt, width), F32),
            pltpu.VMEM((16, key_width), F32),
            pltpu.VMEM((nt, lat + 256), F32),
            pltpu.VMEM((nt, 1, lat + 256), F32),
            pltpu.VMEM((nt, 1, lat + 256), F32),
            pltpu.VMEM((steps, head_count, 1, lat), F32),
            pltpu.VMEM((steps, per, nz, 1, lat), F32),
            pltpu.VMEM((steps, nt, 2 * nz, per // 2 * lat), BF16),
            pltpu.VMEM((1, 1, news), F32),
            pltpu.VMEM((nz, 1, news), F32),
            pltpu.VMEM((nt, 2 * nz, block), BF16),
            pltpu.VMEM((steps, nt * nz, lat), F32),
            pltpu.VMEM((2, nt * nz, depth), BF16),
            pltpu.VMEM((-(-width // 128), nt * nz, 128), F32),
            pltpu.VMEM((nz, nt, width), BF16),
            pltpu.VMEM((nz, nt, width), BF16),
            pltpu.VMEM((nz * nt, width), BF16),
            pltpu.VMEM((side, side, nt, ff + 128), BF16),
            pltpu.VMEM((side, side, nt, ff + 128), BF16),
            pltpu.VMEM((side, nt, ff + 128), BF16),
            pltpu.VMEM((side, nt, ff + 128), BF16),
            pltpu.VMEM((side, side, nt, ff), BF16),
            pltpu.VMEM((side, side, nt, ff), BF16),
            pltpu.VMEM((side, nt, ff), BF16),
            pltpu.VMEM((side, nt, ff), BF16),
            pltpu.VMEM((nt * nt, ff), BF16),
            pltpu.VMEM((nz * nt, width), BF16),
            pltpu.VMEM((nz, nt, width), BF16),
            pltpu.SemaphoreType.DMA((10 + slots // chunk,)),
            pltpu.SemaphoreType.DMA((3,)),
            pltpu.SemaphoreType.DMA((3,)),
            pltpu.SemaphoreType.DMA((11,)),
            pltpu.SemaphoreType.DMA((11,)),
            pltpu.SemaphoreType.DMA((steps,)),
            pltpu.SemaphoreType.DMA((steps,)),
            pltpu.SemaphoreType.DMA((steps,)),
            pltpu.SemaphoreType.DMA((steps,)),
        ],
        compiler_params=pltpu.CompilerParams(
            collective_id=0, has_side_effects=True, vmem_limit_bytes=56 * 1024 * 1024
        ),
        name="decode_layer",
    )(
        token_states,
        queries.reshape(steps, head_count, key_width),
        lengths,
        attn_gain.reshape(1, -1),
        kv_gain.reshape(1, -1),
        mlp_gain.reshape(1, -1),
        jnp.asarray(frequency),
        kv_cache.reshape(slots, key_width).T,
        w_latent,
        w_out.T,
        w_gate_up,
        w_down.T,
    )
    return mixed, latents


def solution(mesh):
    placed = (
        P("dp", "tp"),
        P(None, ("dp", "tp"), None, None),
        P(("dp", "tp"), None, None),
        P(("dp", "tp")),
        P("tp"),
        P(),
        P("tp", None),
        P("dp", "tp"),
        P("tp"),
        P(None, "tp", "dp"),
        P("dp", "tp"),
    )
    return jax.shard_map(
        body,
        mesh=mesh,
        in_specs=placed,
        out_specs=(P(None, "dp", "tp"), P(None, ("dp", "tp"), None)),
        check_vma=False,
    )
```

time: 372 us -> 263 us (0.71)
  Pallas kernels: 354 us -> 258 us
  local copies, waits for them, and re-layouts: 15.3 us -> 2.77 us
    pallas_call x1, Pallas kernels: 354 us -> 258 us  [body(): pl.pallas_call(functools.partial(layer_kernel, float(width * lax.axis_siz...]
    unnamed x22 -> x1, local copies, waits for them, and re-layouts: 14.7 us -> 1.47 us
where the time goes in v2:
time: 263 us; the launch traced here: 262 us
  Pallas kernels  258 us (98%)
  local copies, waits for them, and re-layouts  2.77 us (1%)
    pallas_call x1, Pallas kernels, body(): pl.pallas_call(functools.partial(layer_kernel, float(width * lax.axis_siz...  258 us

profile of v2, /device:TPU:32, one launch (start us, length us, event | category | flops | bytes accessed | tf_op | source)
XLA Modules:
  0.0 262.2 jit_solution(4630280490725877289)
XLA Ops:
  1.3 258.1 %decode_layer.1 = (bf16[4,16,448]{2,1,0:T(8,128)(2,1)}, bf16[4,1,576]{2,1,0:T(2,128)(2,1)}) custom-call(bf16[16,448]{1,0:T(8,128)(2,1)} %x_hbm.1, bf16[4,64,576]{2,1,0:T(8,128)(2,1)} %bitcast.12, s32[1]{0:T(128)S(6)} %copy.16.len_ref, f32[1,448]{1,0:T(1,128)} %bitcast.13, f32[1,512]{1,0:T(1,128)} %bitcast.14, f32[1,448]{1,0:T(1,128)} %bitcast.15, ...), custom_call_target="tpu_custom_call" | custom-call | tf_op jit(solution)/shard_map/decode_layer/pallas_call | solution.py:500
  259.4 1.3 copy.14
  260.7 1.5 copy.17

commit v3 on v2

--- a/solution.py
+++ b/solution.py
@@ -44,6 +44,10 @@
     wo,
     wgu,
     wd,
+    wo_rows,
+    wd_rows,
+    turns,
+    mg_inv,
     scores,
     peak,
     total,
@@ -86,6 +90,7 @@
     o_sent,
     p_sem,
     p_sent,
+    q_sem,
 ):
     nt = x_ref.shape[0]
     nz = nt // 2
@@ -97,6 +102,9 @@
     slots = kv.shape[1]
     per = head_count // nz
     half_per = per // 2
+    cut = ff // 256 * 128
+    middle = (share + 255) // 256 * 128
+    parts = ((0, middle), (middle, share)) if middle < share else ((0, share),)
     chunks = load_sem.shape[0] - 10
     chunk = slots // chunks
     g = lax.axis_index("dp")
@@ -107,20 +115,26 @@
     yy = lax.rem(t, side)
     sibling = (z * 2 + 1 - c, t)
 
-    def z_peer(i):
-        peer = lax.rem(z + i, nz)
+    def away(k, count):
+        odd = lax.rem(k, 2)
+        return count // 2 + k // 2 * (1 - odd) - (k + 1) // 2 * odd
+
+    def z_peer(k):
+        peer = lax.rem(z + away(k, nz), nz)
         return peer, (peer * 2 + c, t)
 
-    def t_peer(i):
-        peer = lax.rem(t + i, nt)
+    def t_peer(k):
+        px = lax.rem(xx + away(k // side, side), side)
+        py = lax.rem(yy + away(lax.rem(k, side), side), side)
+        peer = px * side + py
         return peer, (g, peer)
 
-    def x_peer(i):
-        peer = lax.rem(xx + i, side)
+    def x_peer(k):
+        peer = lax.rem(xx + away(k, side), side)
         return peer, (g, peer * side + yy)
 
-    def y_peer(i):
-        peer = lax.rem(yy + i, side)
+    def y_peer(k):
+        peer = lax.rem(yy + away(k, side), side)
         return peer, (g, xx * side + peer)
 
     def load(source, target, index):
@@ -156,11 +170,11 @@
 
     barrier = pltpu.get_barrier_semaphore()
 
-    @pl.loop(1, nz)
+    @pl.loop(0, nz - 1)
     def _(i):
         pl.semaphore_signal(barrier, inc=1, device_id=z_peer(i)[1], device_id_type=MESH)
 
-    @pl.loop(1, nt)
+    @pl.loop(0, nt - 1)
     def _(i):
         pl.semaphore_signal(barrier, inc=1, device_id=t_peer(i)[1], device_id_type=MESH)
 
@@ -183,7 +197,7 @@
     ]
 
     def send(phase, peer_of, count, source, target):
-        @pl.loop(1, count)
+        @pl.loop(0, count - 1)
         def _(i):
             peer, device = peer_of(i)
             push(source(peer), target, send_sem.at[phase], recv_sem.at[phase], device).start()
@@ -227,51 +241,64 @@
     length = len_ref[0]
     for one in loads[3:]:
         one.wait()
-    queries = q_ref[...].reshape(steps * head_count, key_width)
-    peak[...] = jnp.full_like(peak, -jnp.inf)
-
-    @pl.loop(0, chunks)
-    def _(index):
-        load_kv(index).wait()
-        place = pl.ds(pl.multiple_of(index * chunk, chunk), chunk)
-        part = jnp.dot(queries, kv[:, place], preferred_element_type=F32) * score_scale
-        column = lax.broadcasted_iota(jnp.int32, (1, chunk), 1) + index * chunk
-        part = jnp.where(column < length, part, -jnp.inf)
-        scores[:, place] = part
-        highest = peak[...]
-        for k in range(0, chunk, 128):
-            highest = jnp.maximum(highest, part[:, k : k + 128])
-        peak[...] = highest
-
-    top = jnp.max(peak[...], axis=1, keepdims=True)
-    peak[...] = jnp.broadcast_to(top, peak.shape)
-    total[...] = jnp.zeros_like(total)
-    old[...] = jnp.zeros_like(old)
-
-    @pl.loop(0, chunks)
-    def _(index):
-        place = pl.ds(pl.multiple_of(index * chunk, chunk), chunk)
-        weights = jnp.exp(scores[:, place] - peak[:, :1])
-        running = total[...]
-        for k in range(0, chunk, 128):
-            running = running + weights[:, k : k + 128]
-        total[...] = running
-        old[...] += lax.dot_general(
-            weights.astype(BF16), kv[:lat, place], NT, preferred_element_type=F32
-        )
-
-    total[...] = jnp.broadcast_to(jnp.sum(total[...], axis=1, keepdims=True), total.shape)
-
-    @pl.loop(0, steps)
-    def _(s):
-        rows = pl.ds(pl.multiple_of(s * head_count, head_count), head_count)
+    row = lax.broadcasted_iota(jnp.int32, turns.shape[1:], 0)
+    angles = (row + length).astype(F32) * freq_ref[...]
+    turns[0] = jnp.cos(angles)
+    turns[1] = jnp.sin(angles)
+    mg_inv[...] = 1.0 / mg_ref[...]
+
+    def attend(low, high, arriving):
+        rows = pl.ds(low * head_count, (high - low) * head_count)
+        queries = q_ref[low:high].reshape((high - low) * head_count, key_width)
+        peak[rows, :] = jnp.full((rows.size, 128), -jnp.inf, F32)
+
+        @pl.loop(0, chunks)
+        def _(index):
+            if arriving:
+                load_kv(index).wait()
+            place = pl.ds(pl.multiple_of(index * chunk, chunk), chunk)
+            part = jnp.dot(queries, kv[:, place], preferred_element_type=F32) * score_scale
+            column = lax.broadcasted_iota(jnp.int32, (1, chunk), 1) + index * chunk
+            part = jnp.where(column < length, part, -jnp.inf)
+            scores[rows, place] = part
+            highest = peak[rows, :]
+            for k in range(0, chunk, 128):
+                highest = jnp.maximum(highest, part[:, k : k + 128])
+            peak[rows, :] = highest
+
+        top = jnp.max(peak[rows, :], axis=1, keepdims=True)
+        peak[rows, :] = jnp.broadcast_to(top, (rows.size, 128))
+        total[rows, :] = jnp.zeros((rows.size, 128), F32)
+        old[rows, :] = jnp.zeros((rows.size, lat), F32)
+
+        @pl.loop(0, chunks)
+        def _(index):
+            place = pl.ds(pl.multiple_of(index * chunk, chunk), chunk)
+            weights = jnp.exp(scores[rows, place] - peak[rows, :1])
+            running = total[rows, :]
+            for k in range(0, chunk, 128):
+                running = running + weights[:, k : k + 128]
+            total[rows, :] = running
+            old[rows, :] += lax.dot_general(
+                weights.astype(BF16), kv[:lat, place], NT, preferred_element_type=F32
+            )
+
+        sums = jnp.sum(total[rows, :], axis=1, keepdims=True)
+        total[rows, :] = jnp.broadcast_to(sums, (rows.size, 128))
+
+    def head_rows(s):
+        start = s * head_count
+        return pl.ds(start if isinstance(s, int) else pl.multiple_of(start, head_count), head_count)
+
+    def send_old(s):
+        rows = head_rows(s)
         whole = old[rows, :] / total[rows, :1]
         for h in range(head_count):
             o_send[s, h] = whole[h : h + 1, :]
         mine = pl.ds(z * per, per)
         o_recv[s, :, z] = o_send[s, mine]
 
-        @pl.loop(1, nz)
+        @pl.loop(0, nz - 1)
         def _(i):
             peer, device = z_peer(i)
             theirs = pl.ds(peer * per, per)
@@ -279,26 +306,29 @@
                 o_send.at[s, theirs], o_recv.at[s, :, z], o_sent.at[s], o_sem.at[s], device
             ).start()
 
-    def spread_old(s):
+    wide = half_per * lat // 2
+    sides = [pl.ds(0, wide), pl.ds(wide, wide)]
+
+    def build_old(s):
         await_bytes(o_sem.at[s], o_send.at[s, pl.ds(0, per * (nz - 1))])
         await_bytes(o_sent.at[s], o_send.at[s, pl.ds(0, per * (nz - 1))])
         for h in range(half_per):
             pair = [o_recv[s, k * half_per + h, :, 0, :] for k in range(2)]
             old_heads[s, t, :, h * lat : (h + 1) * lat] = jnp.concatenate(pair, axis=0).astype(BF16)
 
-        @pl.loop(1, nt)
+    def share_old(s, part):
+        @pl.loop(0, nt - 1)
         def _(i):
-            part = old_heads.at[s, t]
-            push(part, part, p_sent.at[s], p_sem.at[s], t_peer(i)[1]).start()
-
-    spread_old(0)
-    for one in own_weights:
-        one.wait()
-    for one in swaps:
-        one.wait()
-
-    @pl.loop(0, steps)
-    def _(s):
+            piece = old_heads.at[s, t, :, sides[part]]
+            push(piece, piece, p_sent.at[2 * s + part], p_sem.at[2 * s + part], t_peer(i)[1]).start()
+
+    def await_old(s, count):
+        for part in range(2):
+            piece = old_heads.at[s, pl.ds(0, count), :, sides[part]]
+            await_bytes(p_sem.at[2 * s + part], piece)
+            await_bytes(p_sent.at[2 * s + part], piece)
+
+    def start_keys(s):
         landed(0, first(a_recv, nt - 1))
         sent(0, first(a_send, nt - 1))
         raw = jnp.sum(a_recv[...], axis=0)
@@ -310,12 +340,11 @@
         rope = raw[:, lat : lat + 128]
         half = (key_width - lat) // 2
         lane = lax.broadcasted_iota(jnp.int32, (1, 128), 1)
-        angles = (length + s).astype(F32) * freq_ref[...]
-        sine = jnp.sin(angles)
         turned = jnp.where(
             lane < half, -pltpu.roll(rope, 128 - half, 1), pltpu.roll(rope, half, 1)
         )
-        rope = rope * jnp.cos(angles) + turned * sine
+        now = pl.ds(s, 1)
+        rope = rope * turns[0, now, :] + turned * turns[1, now, :]
         latent = jnp.concatenate([content, rope], axis=1)[:, :key_width].astype(BF16)
         lat_out[s] = latent
         fresh[pl.ds(s, 1), :] = latent.astype(F32)
@@ -324,7 +353,7 @@
         recent = lax.dot_general(q_ref[s], keys, NT, preferred_element_type=F32) * score_scale
         column = lax.broadcasted_iota(jnp.int32, recent.shape, 1)
         recent = jnp.where(column <= s, recent, -jnp.inf)
-        own = pl.ds(pl.multiple_of(s * head_count, head_count), head_count)
+        own = head_rows(s)
         top_old = peak[own, :1]
         highest = jnp.maximum(top_old, jnp.max(recent, axis=1, keepdims=True))
         weight_old = total[own, :1] * jnp.exp(top_old - highest)
@@ -341,6 +370,7 @@
             b_send[0, :, lat + k * 128 : lat + (k + 1) * 128] = table[k : k + 1, :]
         b_recv[z] = b_send[0]
         send(1, z_peer, nz, lambda peer: b_send.at[0], b_recv.at[z])
+    def share_keys(s):
         landed(1, first(b_recv, nz - 1))
         sent(1, first(b_recv, nz - 1))
         news = b_recv[:, 0, :]
@@ -358,8 +388,55 @@
         lower = jnp.concatenate([news[:, lat // 2 : lat], fine], axis=1)
         l_all[t] = jnp.concatenate([upper, lower], axis=0).astype(BF16)
         send(2, t_peer, nt, lambda peer: l_all.at[t], l_all.at[t])
-        await_bytes(p_sem.at[s], old_heads.at[s, pl.ds(0, nt - 1)])
-        await_bytes(p_sent.at[s], old_heads.at[s, pl.ds(0, nt - 1)])
+    attend(0, 1, True)
+    send_old(0)
+    start_keys(0)
+    build_old(0)
+    first_hop = ((x_peer, sides[0]), (y_peer, sides[1]))
+    for part, (peer_of, cols) in enumerate(first_hop):
+
+        @pl.loop(0, side - 1)
+        def _(i, part=part, peer_of=peer_of, cols=cols):
+            piece = old_heads.at[0, t, :, cols]
+            push(piece, piece, q_sem.at[part], q_sem.at[2 + part], peer_of(i)[1]).start()
+
+    share_keys(0)
+    for part, (_, cols) in enumerate(first_hop):
+        await_bytes(q_sem.at[2 + part], old_heads.at[0, pl.ds(0, side - 1), :, cols])
+        await_bytes(q_sem.at[part], old_heads.at[0, pl.ds(0, side - 1), :, cols])
+
+    @pl.loop(0, side - 1)
+    def _(i):
+        for j in range(side):
+            piece = old_heads.at[0, j * side + yy, :, sides[0]]
+            push(piece, piece, p_sent.at[0], p_sem.at[0], y_peer(i)[1]).start()
+        piece = old_heads.at[0, pl.ds(xx * side, side), :, sides[1]]
+        push(piece, piece, p_sent.at[1], p_sem.at[1], x_peer(i)[1]).start()
+
+    attend(1, steps, False)
+
+    @pl.loop(1, steps)
+    def _(s):
+        send_old(s)
+
+    for one in own_weights:
+        one.wait()
+    for one in swaps:
+        one.wait()
+    for source, target in ((wo, wo_rows), (wd, wd_rows)):
+        size = min(256, source.shape[2] // 2)
+        while source.shape[2] % size:
+            size -= 128
+        for k in range(2):
+
+            @pl.loop(0, source.shape[2] // size)
+            def _(i):
+                place = pl.ds(pl.multiple_of(i * size, size), size)
+                target[k, place, :] = source[k, :, place].T
+    await_old(0, side * (side - 1))
+
+    @pl.loop(0, steps)
+    def _(s):
         landed(2, first(l_all, nt - 1))
         sent(2, first(l_all, nt - 1))
 
@@ -379,96 +456,195 @@
                     joined = joined + latents[j] * table[:, at : at + 1]
                 heads[k, :, h * lat : (h + 1) * lat] = joined.astype(BF16)
 
-        attended = sum(
-            lax.dot_general(heads[k], wo[k], NT, preferred_element_type=F32) for k in range(2)
-        )
-        for k in range(0, share, 128):
-            size = min(128, share - k)
-            y_rows[k // 128, :, :size] = attended[:, k : k + size]
-        for i in range(nz):
-            for k in range(0, share, 128):
-                size = min(128, share - k)
-                picked = y_rows[k // 128, pl.ds(i, nt, stride=nz), :]
-                y_send[i, :, k : k + size] = picked[:, :size].astype(BF16)
-        y_recv[z] = y_send[z]
-        send(3, z_peer, nz, lambda peer: y_send.at[peer], y_recv.at[z])
+        for part, (low, high) in enumerate(parts):
+            cols = pl.ds(low, high - low)
+            attended = sum(
+                jnp.dot(heads[k], wo_rows[k, :, low:high], preferred_element_type=F32)
+                for k in range(2)
+            )
+            for k in range(low, high, 128):
+                size = min(128, high - k)
+                y_rows[k // 128, :, :size] = attended[:, k - low : k - low + size]
+            for i in range(nz):
+                for k in range(low, high, 128):
+                    size = min(128, high - k)
+                    picked = y_rows[k // 128, pl.ds(i, nt, stride=nz), :]
+                    y_send[i, :, k : k + size] = picked[:, :size].astype(BF16)
+            y_recv[z, :, cols] = y_send[z, :, cols]
+            send(
+                3 + part,
+                z_peer,
+                nz,
+                lambda peer, cols=cols: y_send.at[peer, :, cols],
+                y_recv.at[z, :, cols],
+            )
 
         @pl.when(s < steps - 1)
         def _():
-            spread_old(s + 1)
-
-        landed(3, first(y_recv, nz - 1))
-        sent(3, first(y_send, nz - 1))
-        residual = states[...] + jnp.sum(y_recv[...].astype(F32), axis=0)
-        resid[...] = residual
-
-        block(normed, z)[...] = (residual * mg_ref[...]).astype(BF16)
-        send(4, z_peer, nz, lambda peer: block(normed, z), block(normed, z))
-        landed(4, first(normed, nt * (nz - 1)))
-        sent(4, first(normed, nt * (nz - 1)))
+            build_old(s + 1)
+            share_old(s + 1, 0)
+
+        for part, (low, high) in enumerate(parts):
+            cols = pl.ds(low, high - low)
+            landed(3 + part, y_recv.at[pl.ds(0, nz - 1), :, cols])
+            residual = states[:, cols] + jnp.sum(y_recv[:, :, cols].astype(F32), axis=0)
+            resid[:, cols] = residual
+            mine = normed.at[pl.ds(pl.multiple_of(z * nt, nt), nt), cols]
+            mine[...] = (residual * mg_ref[:, cols]).astype(BF16)
+            send(5 + part, z_peer, nz, lambda peer, mine=mine: mine, mine)
+        for part, (low, high) in enumerate(parts):
+            cols = pl.ds(low, high - low)
+            landed(5 + part, normed.at[pl.ds(0, nt * (nz - 1)), cols])
+            sent(3 + part, y_send.at[pl.ds(0, nz - 1), :, cols])
+            sent(5 + part, normed.at[pl.ds(0, nt * (nz - 1)), cols])
 
         rows = normed[...]
-        for k in range(2):
-            gate = jnp.dot(rows, wgu[k, 0], preferred_element_type=F32).astype(BF16)
-            for i in range(nz):
-                place = 2 * i + k
-                gate_send[place // side, place % side, :, :ff] = gate[i * nt : (i + 1) * nt, :]
-        unscaled = rows.astype(F32) / mg_ref[...]
+        unscaled = rows.astype(F32) * mg_inv[...]
         squares = jnp.sum(unscaled * unscaled, axis=1, keepdims=True)
         coarse = squares.astype(BF16).astype(F32)
         lane = lax.broadcasted_iota(jnp.int32, (nt * nz, 128), 1)
-        parts = jnp.where(lane < 64, coarse, squares - coarse).astype(BF16)
+        pair = jnp.where(lane < 64, coarse, squares - coarse).astype(BF16)
         for i in range(nt):
             here = i // 2 * nt
-            gate_send[i // side, i % side, :, ff:] = parts[here : here + nt, :]
-        gate_recv[xx] = gate_send[xx]
-        send(5, x_peer, side, lambda peer: gate_send.at[peer], gate_recv.at[xx])
-        for k in range(2):
-            up = jnp.dot(rows, wgu[k, 1], preferred_element_type=F32).astype(BF16)
-            for i in range(nz):
-                place = 2 * i + k
-                up_send[place % side, place // side] = up[i * nt : (i + 1) * nt, :]
-        up_recv[yy] = up_send[yy]
-        send(6, y_peer, side, lambda peer: up_send.at[peer], up_recv.at[yy])
-        landed(5, first(gate_recv, side - 1))
-        for i in range(side):
-            gate_mid[i] = jnp.sum(gate_recv[:, i].astype(F32), axis=0).astype(BF16)
-        gate_last[yy] = gate_mid[yy]
-        send(7, y_peer, side, lambda peer: gate_mid.at[peer], gate_last.at[yy])
-        landed(6, first(up_recv, side - 1))
-        for i in range(side):
-            up_mid[i] = jnp.sum(up_recv[:, i].astype(F32), axis=0).astype(BF16)
-        up_last[xx] = up_mid[xx]
-        send(8, x_peer, side, lambda peer: up_mid.at[peer], up_last.at[xx])
-        sent(5, first(gate_send, side - 1))
-        sent(6, first(up_send, side - 1))
-        landed(7, first(gate_last, side - 1))
-        gate = jnp.sum(gate_last[...].astype(F32), axis=0)
-        squares = jnp.sum(gate[:, ff:], axis=1, keepdims=True) / 64
-        inverse = lax.rsqrt(squares / width + norm_eps)
-        gate = gate[:, :ff] * inverse
-        gate = gate * jax.nn.sigmoid(gate) * inverse
-        landed(8, first(up_last, side - 1))
-        up = jnp.sum(up_last[...].astype(F32), axis=0)
+            gate_send[i // side, i % side, :, :128] = pair[here : here + nt, :]
+        halves = ((0, cut), (cut, ff))
+        gate_cols = [pl.ds(0, 128 + cut), pl.ds(128 + cut, ff - cut)]
+        up_cols = [pl.ds(0, cut), pl.ds(cut, ff - cut)]
+
+        def three(ref, cols):
+            return ref.at[pl.ds(0, side - 1), :, :, cols]
+
+        def three_mid(ref, cols):
+            return ref.at[pl.ds(0, side - 1), :, cols]
+
+        for part, (low, high) in enumerate(halves):
+            cols = gate_cols[part]
+            for k in range(2):
+                gate = jnp.dot(rows, wgu[k, 0, :, low:high], preferred_element_type=F32)
+                gate = gate.astype(BF16)
+                for i in range(nz):
+                    place = 2 * i + k
+                    gate_send[place // side, place % side, :, 128 + low : 128 + high] = gate[
+                        i * nt : (i + 1) * nt, :
+                    ]
+            gate_recv[xx, :, :, cols] = gate_send[xx, :, :, cols]
+            send(
+                7 + part,
+                x_peer,
+                side,
+                lambda peer, cols=cols: gate_send.at[peer, :, :, cols],
+                gate_recv.at[xx, :, :, cols],
+            )
+            cols = up_cols[part]
+            for k in range(2):
+                up = jnp.dot(rows, wgu[k, 1, :, low:high], preferred_element_type=F32)
+                up = up.astype(BF16)
+                for i in range(nz):
+                    place = 2 * i + k
+                    up_send[place % side, place // side, :, low:high] = up[i * nt : (i + 1) * nt, :]
+            up_recv[yy, :, :, cols] = up_send[yy, :, :, cols]
+            send(
+                9 + part,
+                y_peer,
+                side,
+                lambda peer, cols=cols: up_send.at[peer, :, :, cols],
+                up_recv.at[yy, :, :, cols],
+            )
+        for part in range(2):
+            cols = gate_cols[part]
+            landed(7 + part, three(gate_recv, cols))
+            for i in range(side):
+                gate_mid[i, :, cols] = jnp.sum(gate_recv[:, i, :, cols].astype(F32), axis=0).astype(
+                    BF16
+                )
+            gate_last[yy, :, cols] = gate_mid[yy, :, cols]
+            send(
+                11 + part,
+                y_peer,
+                side,
+                lambda peer, cols=cols: gate_mid.at[peer, :, cols],
+                gate_last.at[yy, :, cols],
+            )
+            cols = up_cols[part]
+            landed(9 + part, three(up_recv, cols))
+            for i in range(side):
+                up_mid[i, :, cols] = jnp.sum(up_recv[:, i, :, cols].astype(F32), axis=0).astype(
+                    BF16
+                )
+            up_last[xx, :, cols] = up_mid[xx, :, cols]
+            send(
+                13 + part,
+                x_peer,
+                side,
+                lambda peer, cols=cols: up_mid.at[peer, :, cols],
+                up_last.at[xx, :, cols],
+            )
         place = lax.rem(t, 2) * nz + t // 2
-        block(hidden, place)[...] = (gate * up).astype(BF16)
-        send(9, t_peer, nt, lambda peer: block(hidden, place), block(hidden, place))
-        sent(7, first(gate_mid, side - 1))
-        sent(8, first(up_mid, side - 1))
-        landed(9, first(hidden, nt * (nt - 1)))
-        sent(9, first(hidden, nt * (nt - 1)))
-
-        down = sum(
-            lax.dot_general(
-                hidden[k * nz * nt : (k + 1) * nz * nt, :], wd[k], NT, preferred_element_type=F32
+        inverse = None
+        for part, (low, high) in enumerate(halves):
+            cols = gate_cols[part]
+            landed(11 + part, three_mid(gate_last, cols))
+            gate = jnp.sum(gate_last[:, :, cols].astype(F32), axis=0)
+            if part == 0:
+                squares = jnp.sum(gate[:, :128], axis=1, keepdims=True) / 64
+                inverse = lax.rsqrt(squares / width + norm_eps)
+                gate = gate[:, 128:]
+            gate = gate * inverse
+            gate = gate * jax.nn.sigmoid(gate) * inverse
+            cols = up_cols[part]
+            landed(13 + part, three_mid(up_last, cols))
+            up = jnp.sum(up_last[:, :, cols].astype(F32), axis=0)
+            mine = hidden.at[pl.ds(pl.multiple_of(place * nt, nt), nt), cols]
+            mine[...] = (gate * up).astype(BF16)
+            send(15 + part, t_peer, nt, lambda peer, mine=mine: mine, mine)
+        for part in range(2):
+            sent(7 + part, three(gate_send, gate_cols[part]))
+            sent(9 + part, three(up_send, up_cols[part]))
+            sent(11 + part, three_mid(gate_mid, gate_cols[part]))
+            sent(13 + part, three_mid(up_mid, up_cols[part]))
+
+        landed(15, hidden.at[pl.ds(0, nt * (nt - 1)), up_cols[0]])
+        half_rows = nz * nt
+        early = sum(
+            jnp.dot(
+                hidden[k * half_rows : (k + 1) * half_rows, :cut],
+                wd_rows[k, :cut, :],
+                preferred_element_type=F32,
             )
             for k in range(2)
         )
-        d_send[...] = down.astype(BF16)
-        d_recv[z] = block(d_send, z)[...]
-        send(10, z_peer, nz, lambda peer: block(d_send, peer), d_recv.at[z])
-        landed(10, first(d_recv, nz - 1))
-        sent(10, first(d_recv, nz - 1))
+        landed(16, hidden.at[pl.ds(0, nt * (nt - 1)), up_cols[1]])
+        for part, (low, high) in enumerate(parts):
+            cols = pl.ds(low, high - low)
+            down = early[:, low:high] + sum(
+                jnp.dot(
+                    hidden[k * half_rows : (k + 1) * half_rows, cut:],
+                    wd_rows[k, cut:, low:high],
+                    preferred_element_type=F32,
+                )
+                for k in range(2)
+            )
+            d_send[:, cols] = down.astype(BF16)
+            d_recv[z, :, cols] = d_send[pl.ds(pl.multiple_of(z * nt, nt), nt), cols]
+            send(
+                17 + part,
+                z_peer,
+                nz,
+                lambda peer, cols=cols: d_send.at[
+                    pl.ds(pl.multiple_of(peer * nt, nt), nt), cols
+                ],
+                d_recv.at[z, :, cols],
+            )
+        @pl.when(s < steps - 1)
+        def _():
+            share_old(s + 1, 1)
+
+        for part in range(2):
+            sent(15 + part, hidden.at[pl.ds(0, nt * (nt - 1)), up_cols[part]])
+        for part, (low, high) in enumerate(parts):
+            cols = pl.ds(low, high - low)
+            landed(17 + part, d_recv.at[pl.ds(0, nz - 1), :, cols])
+            sent(17 + part, d_send.at[pl.ds(0, nt * (nz - 1)), cols])
         mixed = (resid[...] + jnp.sum(d_recv[...].astype(F32), axis=0)).astype(BF16)
         out_ref[s] = mixed
         states[...] = mixed.astype(F32)
@@ -476,6 +652,9 @@
         @pl.when(s < steps - 1)
         def _():
             send_latent()
+            start_keys(s + 1)
+            share_keys(s + 1)
+            await_old(s + 1, nt - 1)
 
 
 def body(token_states, queries, kv_cache, lengths, attn_gain, kv_gain, w_latent, w_out, mlp_gain, w_gate_up, w_down):
@@ -517,6 +696,10 @@
             pltpu.VMEM((2, width, depth), BF16),
             pltpu.VMEM((2,) + w_gate_up.shape, BF16),
             pltpu.VMEM((2, width, ff), BF16),
+            pltpu.VMEM((2, depth, width), BF16),
+            pltpu.VMEM((2, ff, width), BF16),
+            pltpu.VMEM((2, 8, 128), F32),
+            pltpu.VMEM((1, width), F32),
             pltpu.VMEM((rows, slots), F32),
             pltpu.VMEM((rows, 128), F32),
             pltpu.VMEM((rows, 128), F32),
@@ -553,12 +736,13 @@
             pltpu.SemaphoreType.DMA((10 + slots // chunk,)),
             pltpu.SemaphoreType.DMA((3,)),
             pltpu.SemaphoreType.DMA((3,)),
-            pltpu.SemaphoreType.DMA((11,)),
-            pltpu.SemaphoreType.DMA((11,)),
+            pltpu.SemaphoreType.DMA((19,)),
+            pltpu.SemaphoreType.DMA((19,)),
             pltpu.SemaphoreType.DMA((steps,)),
             pltpu.SemaphoreType.DMA((steps,)),
-            pltpu.SemaphoreType.DMA((steps,)),
-            pltpu.SemaphoreType.DMA((steps,)),
+            pltpu.SemaphoreType.DMA((2 * steps,)),
+            pltpu.SemaphoreType.DMA((2 * steps,)),
+            pltpu.SemaphoreType.DMA((4,)),
         ],
         compiler_params=pltpu.CompilerParams(
             collective_id=0, has_side_effects=True, vmem_limit_bytes=56 * 1024 * 1024

time: 263 us -> 233 us (0.89)
  Pallas kernels: 258 us -> 229 us
    pallas_call x1, Pallas kernels: 258 us -> 229 us  [body(): pl.pallas_call(functools.partial(layer_kernel, float(width * lax.axis_siz...]
where the time goes in v3:
time: 233 us
  Pallas kernels  229 us (98%)
  local copies, waits for them, and re-layouts  2.77 us (1%)
    pallas_call x1, Pallas kernels, body(): pl.pallas_call(functools.partial(layer_kernel, float(width * lax.axis_siz...  229 us

profile of v3, /device:TPU:32, one launch (start us, length us, event | category | flops | bytes accessed | tf_op | source)
XLA Modules:
  0.0 233.0 jit_solution(6246543973903651045)
XLA Ops:
  1.3 228.9 %decode_layer.1 = (bf16[4,16,448]{2,1,0:T(8,128)(2,1)}, bf16[4,1,576]{2,1,0:T(2,128)(2,1)}) custom-call(bf16[16,448]{1,0:T(8,128)(2,1)} %x_hbm.1, bf16[4,64,576]{2,1,0:T(8,128)(2,1)} %bitcast.12, s32[1]{0:T(128)S(6)} %copy.16.len_ref, f32[1,448]{1,0:T(1,128)} %bitcast.13, f32[1,512]{1,0:T(1,128)} %bitcast.14, f32[1,448]{1,0:T(1,128)} %bitcast.15, ...), custom_call_target="tpu_custom_call" | custom-call | tf_op jit(solution)/shard_map/decode_layer/pallas_call | solution.py:679
  230.2 1.3 copy.14
  231.5 1.5 copy.17

commit v4 on v3

--- a/solution.py
+++ b/solution.py
@@ -51,6 +51,8 @@
     scores,
     peak,
     total,
+    peak_rows,
+    total_rows,
     old,
     states,
     resid,
@@ -231,6 +233,7 @@
     a_rows[...] = jnp.zeros_like(a_rows)
     fresh[...] = jnp.zeros_like(fresh)
     latents[...] = jnp.zeros_like(latents)
+    b_send[...] = jnp.zeros_like(b_send)
     for one in loads[:3]:
         one.wait()
     states[...] = x_ref[...].astype(F32)
@@ -285,6 +288,11 @@
 
         sums = jnp.sum(total[rows, :], axis=1, keepdims=True)
         total[rows, :] = jnp.broadcast_to(sums, (rows.size, 128))
+        rest = jnp.zeros((128 - head_count, 128), F32)
+        for s in range(low, high):
+            here = pl.ds(s * head_count, head_count)
+            peak_rows[s] = jnp.concatenate([peak[here, :], rest], axis=0).T[:1, :]
+            total_rows[s] = jnp.concatenate([total[here, :], rest], axis=0).T[:1, :]
 
     def head_rows(s):
         start = s * head_count
@@ -346,28 +354,23 @@
         now = pl.ds(s, 1)
         rope = rope * turns[0, now, :] + turned * turns[1, now, :]
         latent = jnp.concatenate([content, rope], axis=1)[:, :key_width].astype(BF16)
-        lat_out[s] = latent
         fresh[pl.ds(s, 1), :] = latent.astype(F32)
 
         keys = fresh[...].astype(BF16)
-        recent = lax.dot_general(q_ref[s], keys, NT, preferred_element_type=F32) * score_scale
-        column = lax.broadcasted_iota(jnp.int32, recent.shape, 1)
-        recent = jnp.where(column <= s, recent, -jnp.inf)
-        own = head_rows(s)
-        top_old = peak[own, :1]
-        highest = jnp.maximum(top_old, jnp.max(recent, axis=1, keepdims=True))
-        weight_old = total[own, :1] * jnp.exp(top_old - highest)
+        recent = lax.dot_general(keys, q_ref[s], NT, preferred_element_type=F32) * score_scale
+        place = lax.broadcasted_iota(jnp.int32, recent.shape, 0)
+        recent = jnp.where(place <= s, recent, -jnp.inf)
+        top_old = peak_rows[s, :, :head_count]
+        highest = jnp.maximum(top_old, jnp.max(recent, axis=0, keepdims=True))
+        weight_old = total_rows[s, :, :head_count] * jnp.exp(top_old - highest)
         weight_new = jnp.exp(recent - highest)
-        denominator = weight_old + jnp.sum(weight_new, axis=1, keepdims=True)
+        denominator = weight_old + jnp.sum(weight_new, axis=0, keepdims=True)
         share_new = (weight_new / denominator).astype(BF16).astype(F32)
-        column = lax.broadcasted_iota(jnp.int32, (head_count, 128), 1)
-        table = jnp.where(column == 0, weight_old / denominator, 0.0)
-        for j in range(steps):
-            table = jnp.where(column == j + 1, share_new[:, j : j + 1], table)
-        table = jnp.concatenate([table, jnp.zeros((128 - head_count, 128), F32)], axis=0).T
         b_send[0, :, :lat] = latent[:, :lat].astype(F32)
-        for k in range(steps + 1):
-            b_send[0, :, lat + k * 128 : lat + (k + 1) * 128] = table[k : k + 1, :]
+        b_send[0, :, lat : lat + head_count] = weight_old / denominator
+        for k in range(steps):
+            start = lat + (k + 1) * 128
+            b_send[0, :, start : start + head_count] = share_new[k : k + 1, :]
         b_recv[z] = b_send[0]
         send(1, z_peer, nz, lambda peer: b_send.at[0], b_recv.at[z])
     def share_keys(s):
@@ -656,6 +659,17 @@
             share_keys(s + 1)
             await_old(s + 1, nt - 1)
 
+    lat_out[...] = fresh[:steps, :].astype(BF16)
+
+
+def hand_out(mixed_ref, lat_ref, mixed_hbm, lat_hbm, sem):
+    one = pltpu.make_async_copy(mixed_ref, mixed_hbm, sem.at[0])
+    two = pltpu.make_async_copy(lat_ref, lat_hbm, sem.at[1])
+    one.start()
+    two.start()
+    one.wait()
+    two.wait()
+
 
 def body(token_states, queries, kv_cache, lengths, attn_gain, kv_gain, w_latent, w_out, mlp_gain, w_gate_up, w_down):
     nt, width = token_states.shape
@@ -670,7 +684,7 @@
     half = (key_width - lat) // 2
     frequency = np.zeros((1, 128), np.float32)
     frequency[0, : 2 * half] = np.tile(10000.0 ** (-np.arange(half) / half), 2)
-    chunk = min(512, slots)
+    chunk = min(1024, slots)
     rows = steps * head_count
     vmem = pl.BlockSpec(memory_space=pltpu.VMEM)
     hbm = pl.BlockSpec(memory_space=pl.ANY)
@@ -680,7 +694,7 @@
         functools.partial(layer_kernel, float(width * lax.axis_size("tp"))),
         out_shape=(
             jax.ShapeDtypeStruct((steps, nt, width), BF16),
-            jax.ShapeDtypeStruct((steps, 1, key_width), BF16),
+            jax.ShapeDtypeStruct((steps, key_width), BF16),
         ),
         in_specs=[hbm, hbm, pl.BlockSpec(memory_space=pltpu.SMEM)] + [hbm] * 9,
         out_specs=(vmem, vmem),
@@ -703,6 +717,8 @@
             pltpu.VMEM((rows, slots), F32),
             pltpu.VMEM((rows, 128), F32),
             pltpu.VMEM((rows, 128), F32),
+            pltpu.VMEM((steps, 1, 128), F32),
+            pltpu.VMEM((steps, 1, 128), F32),
             pltpu.VMEM((rows, lat), F32),
             pltpu.VMEM((nt, width), F32),
             pltpu.VMEM((nt, width), F32),
@@ -762,7 +778,7 @@
         w_gate_up,
         w_down.T,
     )
-    return mixed, latents
+    return mixed, latents.reshape(steps, 1, key_width)
 
 
 def solution(mesh):

time: 233 us -> 231 us (level)
  no operation moved by 1% of the time
where the time goes in v4:
time: 231 us
  Pallas kernels  227 us (98%)
  local copies, waits for them, and re-layouts  2.76 us (1%)
    pallas_call x1, Pallas kernels, body(): pl.pallas_call(functools.partial(layer_kernel, float(width * lax.axis_siz...  227 us

profile of v4, /device:TPU:32, one launch (start us, length us, event | category | flops | bytes accessed | tf_op | source)
XLA Modules:
  0.0 231.1 jit_solution(43634049616061311)
XLA Ops:
  1.3 227.1 %decode_layer.1 = (bf16[4,16,448]{2,1,0:T(8,128)(2,1)}, bf16[4,576]{1,0:T(4,128)(2,1)}) custom-call(bf16[16,448]{1,0:T(8,128)(2,1)} %x_hbm.1, bf16[4,64,576]{2,1,0:T(8,128)(2,1)} %bitcast.13, s32[1]{0:T(128)S(6)} %copy.16.len_ref, f32[1,448]{1,0:T(1,128)} %bitcast.15, f32[1,512]{1,0:T(1,128)} %bitcast.16, f32[1,448]{1,0:T(1,128)} %bitcast.17, ...), custom_call_target="tpu_custom_call" | custom-call | tf_op jit(solution)/shard_map/decode_layer/pallas_call | solution.py:693
  228.3 1.5 copy.17
  229.8 1.3 copy.18

commit v5 on v4

--- a/solution.py
+++ b/solution.py
@@ -167,8 +167,6 @@
         load(wgu_hbm, wgu.at[c], 8),
         load(wd_hbm, wd.at[c], 9),
     ]
-    for one in own_weights:
-        one.start()
 
     barrier = pltpu.get_barrier_semaphore()
 
@@ -238,8 +236,6 @@
         one.wait()
     states[...] = x_ref[...].astype(F32)
     send_latent()
-    for one in swaps:
-        one.start()
 
     length = len_ref[0]
     for one in loads[3:]:
@@ -394,6 +390,8 @@
     attend(0, 1, True)
     send_old(0)
     start_keys(0)
+    for one in own_weights + swaps:
+        one.start()
     build_old(0)
     first_hop = ((x_peer, sides[0]), (y_peer, sides[1]))
     for part, (peer_of, cols) in enumerate(first_hop):

time: 231 us -> 230 us (level)
  no operation moved by 1% of the time
where the time goes in v5:
time: 230 us
  Pallas kernels  226 us (98%)
  local copies, waits for them, and re-layouts  2.76 us (1%)
    pallas_call x1, Pallas kernels, body(): pl.pallas_call(functools.partial(layer_kernel, float(width * lax.axis_siz...  226 us

profile of v5, /device:TPU:32, one launch (start us, length us, event | category | flops | bytes accessed | tf_op | source)
XLA Modules:
  0.0 230.0 jit_solution(13099874597317795987)
XLA Ops:
  1.3 225.9 %decode_layer.1 = (bf16[4,16,448]{2,1,0:T(8,128)(2,1)}, bf16[4,576]{1,0:T(4,128)(2,1)}) custom-call(bf16[16,448]{1,0:T(8,128)(2,1)} %x_hbm.1, bf16[4,64,576]{2,1,0:T(8,128)(2,1)} %bitcast.13, s32[1]{0:T(128)S(6)} %copy.16.len_ref, f32[1,448]{1,0:T(1,128)} %bitcast.15, f32[1,512]{1,0:T(1,128)} %bitcast.16, f32[1,448]{1,0:T(1,128)} %bitcast.17, ...), custom_call_target="tpu_custom_call" | custom-call | tf_op jit(solution)/shard_map/decode_layer/pallas_call | solution.py:691
  227.2 1.5 copy.17
  228.7 1.3 copy.18
